TPU v7x, 512 devices: a whole 4x4x16 slice. The times are simulated.
512 devices in a mesh: context: 64 (over x, z), tensor: 8 (over y, core).
Axes of the slice: x: 4, y: 4, z: 16, core: 2. Of those that a mesh axis runs over, the one named last changes fastest.
Arguments:
- sequence: bfloat16 [256, 32768], P('tensor', 'context'), may hold values from -6 to 6
- proj_in: bfloat16 [3, 256, 256], P(None, None, 'tensor'), may hold values from -0.375 to 0.375
- conv_filter: float32 [256, 32768], P('tensor', 'context'), may hold values from -2 to 2
- skip_gain: float32 [256], P('tensor'), may hold values from -1 to 1
- proj_out: bfloat16 [256, 256], P('tensor'), may hold values from -0.375 to 0.375
Outputs:
- mixed_out: bfloat16 [256, 32768], P(None, 'context')
All inputs are finite; a program needn't handle non-finite values.
Results may differ from a plain program's by a relative error of at most 0.0049.
Values may be sent and summed in bfloat16 or wider, within the bound.
No kernel may reach another device: no remote copies, remote signals or barrier semaphores. Data moves between devices by JAX's collectives and lax.ppermute only.
A program may use at most 64 MiB of HBM per device.

v0:
```python
import math

import jax
import jax.numpy as jnp
from jax import lax
from jax.sharding import PartitionSpec as P

HIGHEST_MODE = lax.Precision.HIGHEST


def swapped(value, axis, apart):
    mask = 2**apart
    pairs = [(source, source ^ mask) for source in range(lax.axis_size(axis))]
    return lax.ppermute(value, axis, pairs)


def angles(exponent, period):
    radians = (exponent % period).astype(jnp.float32) * (2.0 * math.pi / period)
    return (jnp.cos(radians), jnp.sin(radians))


def rotate(signal, cos_part, sin_part):
    return jnp.stack(
        [signal[0] * cos_part - signal[1] * sin_part, signal[0] * sin_part + signal[1] * cos_part]
    )


def apply_table(signal, cos_part, sin_part, pattern):
    real_part = jnp.einsum(pattern, signal[0], cos_part, precision=HIGHEST_MODE) - jnp.einsum(
        pattern, signal[1], sin_part, precision=HIGHEST_MODE
    )
    imag_part = jnp.einsum(pattern, signal[0], sin_part, precision=HIGHEST_MODE) + jnp.einsum(
        pattern, signal[1], cos_part, precision=HIGHEST_MODE
    )
    return jnp.stack([real_part, imag_part])


def local_forward(signal):
    streams, channels, tok_len = signal.shape[1:]
    inner_len = min(128, tok_len)
    outer_len = tok_len // inner_len
    blocks = signal.reshape(2, streams, channels, outer_len, inner_len)
    outer_idx = jnp.arange(outer_len, dtype=jnp.int32)
    inner_idx = jnp.arange(inner_len, dtype=jnp.int32)
    cos_part, sin_part = angles(outer_idx[:, None] * outer_idx[None, :], outer_len)
    blocks = apply_table(blocks, cos_part, -sin_part, "sdab,am->sdmb")
    cos_part, sin_part = angles(outer_idx[:, None] * inner_idx[None, :], tok_len)
    blocks = rotate(blocks, cos_part, -sin_part)
    cos_part, sin_part = angles(inner_idx[:, None] * inner_idx[None, :], inner_len)
    blocks = apply_table(blocks, cos_part, -sin_part, "sdmb,bn->sdmn")
    return blocks.reshape(2, streams, channels, tok_len)


def local_inverse(signal):
    streams, channels, tok_len = signal.shape[1:]
    inner_len = min(128, tok_len)
    outer_len = tok_len // inner_len
    blocks = signal.reshape(2, streams, channels, outer_len, inner_len)
    outer_idx = jnp.arange(outer_len, dtype=jnp.int32)
    inner_idx = jnp.arange(inner_len, dtype=jnp.int32)
    cos_part, sin_part = angles(inner_idx[:, None] * inner_idx[None, :], inner_len)
    blocks = apply_table(blocks, cos_part, sin_part, "sdmn,nb->sdmb")
    cos_part, sin_part = angles(outer_idx[:, None] * inner_idx[None, :], tok_len)
    blocks = rotate(blocks, cos_part, sin_part)
    cos_part, sin_part = angles(outer_idx[:, None] * outer_idx[None, :], outer_len)
    blocks = apply_table(blocks, cos_part, sin_part, "sdmb,ma->sdab")
    return blocks.reshape(2, streams, channels, tok_len)


def shards(sequence, proj_in, conv_filter, skip_gain, proj_out):
    tok_len = sequence.shape[1]
    context_size = lax.axis_size("context")
    context_rank = lax.axis_index("context")
    length = tok_len * context_size
    sections = context_size.bit_length() - 1
    projected = jnp.einsum(
        "bio,il->bol",
        proj_in,
        lax.all_gather(sequence, "tensor", axis=0, tiled=True),
        preferred_element_type=jnp.float32,
    )
    gated_value = projected[2] * projected[0]
    offsets = jnp.arange(tok_len, dtype=jnp.int32)
    position = context_rank * tok_len + offsets
    pad_cos, pad_sin = angles(position, 2 * length)
    blank = jnp.zeros_like(gated_value)
    real_part = jnp.stack([gated_value, gated_value * pad_cos, conv_filter, conv_filter * pad_cos])
    imag_part = jnp.stack([blank, -gated_value * pad_sin, blank, -conv_filter * pad_sin])
    signal = jnp.stack([real_part, imag_part])
    for bit_pos in reversed(range(sections)):
        partner = swapped(signal, "context", bit_pos)
        is_upper = context_rank // (1 << bit_pos) % 2 == 1
        cos_part, sin_part = angles(
            context_rank % (1 << bit_pos) * tok_len + offsets, 2 * (1 << bit_pos) * tok_len
        )
        signal = jnp.where(
            is_upper, rotate(partner - signal, cos_part, -sin_part), signal + partner
        )
    spectra = local_forward(signal)
    source = spectra[:, 0:2]
    response = spectra[:, 2:4]
    product = jnp.stack(
        [
            source[0] * response[0] - source[1] * response[1],
            source[0] * response[1] + source[1] * response[0],
        ]
    )
    signal = local_inverse(product)
    for bit_pos in range(sections):
        is_upper = context_rank // (1 << bit_pos) % 2 == 1
        cos_part, sin_part = angles(
            context_rank % (1 << bit_pos) * tok_len + offsets, 2 * (1 << bit_pos) * tok_len
        )
        turned = jnp.where(is_upper, rotate(signal, cos_part, sin_part), signal)
        partner = swapped(turned, "context", bit_pos)
        signal = jnp.where(is_upper, partner - turned, signal + partner)
    convolved = (signal[0, 0] + signal[0, 1] * pad_cos - signal[1, 1] * pad_sin) / (2.0 * length)
    convolved = convolved + skip_gain[:, None] * gated_value
    out_gated = (convolved * projected[1]).astype(jnp.bfloat16)
    partial_terms = jnp.einsum("io,il->ol", proj_out, out_gated, preferred_element_type=jnp.float32)
    mixed_out = lax.psum(partial_terms, "tensor").astype(jnp.bfloat16)
    return mixed_out


def solution(mesh):
    return jax.shard_map(
        shards,
        mesh=mesh,
        in_specs=(
            P("tensor", "context"),
            P(None, None, "tensor"),
            P("tensor", "context"),
            P("tensor"),
            P("tensor", None),
        ),
        out_specs=P(None, "context"),
        check_vma=False,
    )
```

profile of v0, /device:TPU:1, one launch (start us, length us, event | category | flops | bytes accessed | tf_op | source)
XLA Modules:
  0.0 340.3 jit_solution(7092914386189817224)
XLA Ops:
  0.1 19.8 %all_gather.3 = bf16[256,512]{1,0:T(8,128)(2,1)S(1)} all-gather(bf16[32,512]{1,0:T(8,128)(2,1)} %param.5), channel_id=1, replica_groups=mesh['context'=64,'tensor'=8] {'tensor'}, dimensions={0}, use_global_device_ids=true | all-gather | bytes 294912 | tf_op jit(solution)/shard_map/all_gather | solution.py:79
  20.1 0.8 copy-done.1
  21.0 1.9 collective-permute-start
  23.1 14.7 %collective-permute-done = f32[2,4,32,512]{3,2,1,0:T(8,128)S(1)} collective-permute-done((f32[2,4,32,512]{3,2,1,0:T(8,128)S(1)}, f32[2,4,32,512]{3,2,1,0:T(8,128)S(1)}, u32[]{:S(2)}, u32[]{:S(2)}) %collective-permute-start) | collective-permute-done | bytes 524320 | tf_op jit(solution)/shard_map/ppermute | solution.py:14
  38.1 1.9 collective-permute-start.1
  40.2 12.3 %collective-permute-done.1 = f32[2,4,32,512]{3,2,1,0:T(8,128)S(1)} collective-permute-done((f32[2,4,32,512]{3,2,1,0:T(8,128)S(1)}, f32[2,4,32,512]{3,2,1,0:T(8,128)S(1)}, u32[]{:S(2)}, u32[]{:S(2)}) %collective-permute-start.1) | collective-permute-done | bytes 524320 | tf_op jit(solution)/shard_map/ppermute | solution.py:14
  52.5 0.2 fusion.210
  52.8 0.3 maximum_select_fusion.1
  53.1 10.6 %collective-permute-start.2 = (f32[2,4,32,512]{3,2,1,0:T(8,128)S(1)}, f32[2,4,32,512]{3,2,1,0:T(8,128)S(1)}, u32[]{:S(2)}, u32[]{:S(2)}) collective-permute-start(f32[2,4,32,512]{3,2,1,0:T(8,128)S(1)} %maximum_select_fusion.1), channel_id=1, source_target_pairs={{0,64},{8,72},{16,80},{24,88},{32,96},{40,104},{48,112},{56,120},{... | collective-permute-start | bytes 1572872 | tf_op jit(solution)/shard_map/ppermute | solution.py:14
  63.8 23.8 %collective-permute-done.2 = f32[2,4,32,512]{3,2,1,0:T(8,128)S(1)} collective-permute-done((f32[2,4,32,512]{3,2,1,0:T(8,128)S(1)}, f32[2,4,32,512]{3,2,1,0:T(8,128)S(1)}, u32[]{:S(2)}, u32[]{:S(2)}) %collective-permute-start.2) | collective-permute-done | bytes 524320 | tf_op jit(solution)/shard_map/ppermute | solution.py:14
  87.9 19.3 %collective-permute-start.3 = (f32[2,4,32,512]{3,2,1,0:T(8,128)S(1)}, f32[2,4,32,512]{3,2,1,0:T(8,128)S(1)}, u32[]{:S(2)}, u32[]{:S(2)}) collective-permute-start(f32[2,4,32,512]{3,2,1,0:T(8,128)S(1)} %maximum_select_fusion.2), channel_id=1, source_target_pairs={{0,32},{8,40},{16,48},{24,56},{32,0},{40,8},{48,16},{56,24},{64,96... | collective-permute-start | bytes 1572872 | tf_op jit(solution)/shard_map/ppermute | solution.py:14
  107.3 48.0 %collective-permute-done.3 = f32[2,4,32,512]{3,2,1,0:T(8,128)S(1)} collective-permute-done((f32[2,4,32,512]{3,2,1,0:T(8,128)S(1)}, f32[2,4,32,512]{3,2,1,0:T(8,128)S(1)}, u32[]{:S(2)}, u32[]{:S(2)}) %collective-permute-start.3) | collective-permute-done | bytes 524320 | tf_op jit(solution)/shard_map/ppermute | solution.py:14
  155.7 1.9 collective-permute-start.4
  157.7 23.6 %collective-permute-done.4 = f32[2,4,32,512]{3,2,1,0:T(8,128)S(1)} collective-permute-done((f32[2,4,32,512]{3,2,1,0:T(8,128)S(1)}, f32[2,4,32,512]{3,2,1,0:T(8,128)S(1)}, u32[]{:S(2)}, u32[]{:S(2)}) %collective-permute-start.4) | collective-permute-done | bytes 524320 | tf_op jit(solution)/shard_map/ppermute | solution.py:14
  181.6 2.1 collective-permute-start.5
  183.9 12.6 %collective-permute-done.5 = f32[2,4,32,512]{3,2,1,0:T(8,128)S(1)} collective-permute-done((f32[2,4,32,512]{3,2,1,0:T(8,128)S(1)}, f32[2,4,32,512]{3,2,1,0:T(8,128)S(1)}, u32[]{:S(2)}, u32[]{:S(2)}) %collective-permute-start.5) | collective-permute-done | bytes 524320 | tf_op jit(solution)/shard_map/ppermute | solution.py:14
  197.0 0.6 fusion.90
  197.6 0.6 fusion.94
  198.3 0.6 convolution_subtract_fusion.1
  198.9 0.7 add_bitcast_fusion
  199.6 0.6 fusion.8
  200.3 0.6 fusion.6
  200.9 0.6 convolution_subtract_fusion
  201.8 0.6 convolution_add_fusion
  202.4 0.2 copy.20
  202.8 0.5 fusion.14
  203.3 0.5 fusion.12
  203.9 0.5 convolution_subtract_fusion.3
  204.4 0.5 multiply_add_fusion.12
  204.9 0.4 fusion.20
  205.4 0.4 fusion.18
  205.8 0.4 fusion.1
  206.3 0.4 fusion
  206.9 2.2 collective-permute-start.6
  209.2 6.1 %collective-permute-done.6 = f32[2,2,32,512]{3,2,1,0:T(8,128)S(1)} collective-permute-done((f32[2,2,32,512]{3,2,1,0:T(8,128)S(1)}, f32[2,2,32,512]{3,2,1,0:T(8,128)S(1)}, u32[]{:S(2)}, u32[]{:S(2)}) %collective-permute-start.6) | collective-permute-done | bytes 262176 | tf_op jit(solution)/shard_map/ppermute | solution.py:14
  215.4 1.9 collective-permute-start.7
  217.4 14.2 %collective-permute-done.7 = f32[2,2,32,512]{3,2,1,0:T(8,128)S(1)} collective-permute-done((f32[2,2,32,512]{3,2,1,0:T(8,128)S(1)}, f32[2,2,32,512]{3,2,1,0:T(8,128)S(1)}, u32[]{:S(2)}, u32[]{:S(2)}) %collective-permute-start.7) | collective-permute-done | bytes 262176 | tf_op jit(solution)/shard_map/ppermute | solution.py:14
  231.8 1.9 collective-permute-start.8
  233.8 26.0 %collective-permute-done.8 = f32[2,2,32,512]{3,2,1,0:T(8,128)S(1)} collective-permute-done((f32[2,2,32,512]{3,2,1,0:T(8,128)S(1)}, f32[2,2,32,512]{3,2,1,0:T(8,128)S(1)}, u32[]{:S(2)}, u32[]{:S(2)}) %collective-permute-start.8) | collective-permute-done | bytes 262176 | tf_op jit(solution)/shard_map/ppermute | solution.py:14
  259.9 15.1 %collective-permute-start.9 = (f32[2,2,32,512]{3,2,1,0:T(8,128)S(1)}, f32[2,2,32,512]{3,2,1,0:T(8,128)S(1)}, u32[]{:S(2)}, u32[]{:S(2)}) collective-permute-start(f32[2,2,32,512]{3,2,1,0:T(8,128)S(1)} %maximum_select_fusion.9), channel_id=1, source_target_pairs={{0,64},{8,72},{16,80},{24,88},{32,96},{40,104},{48,112},{56,120},{... | collective-permute-start | bytes 786440 | tf_op jit(solution)/shard_map/ppermute | solution.py:14
  275.1 15.4 %collective-permute-done.9 = f32[2,2,32,512]{3,2,1,0:T(8,128)S(1)} collective-permute-done((f32[2,2,32,512]{3,2,1,0:T(8,128)S(1)}, f32[2,2,32,512]{3,2,1,0:T(8,128)S(1)}, u32[]{:S(2)}, u32[]{:S(2)}) %collective-permute-start.9) | collective-permute-done | bytes 262176 | tf_op jit(solution)/shard_map/ppermute | solution.py:14
  290.7 4.3 %collective-permute-start.10 = (f32[2,2,32,512]{3,2,1,0:T(8,128)S(1)}, f32[2,2,32,512]{3,2,1,0:T(8,128)S(1)}, u32[]{:S(2)}, u32[]{:S(2)}) collective-permute-start(f32[2,2,32,512]{3,2,1,0:T(8,128)S(1)} %maximum_select_fusion.10), channel_id=1, source_target_pairs={{0,128},{8,136},{16,144},{24,152},{32,160},{40,168},{48,176},{56,1... | collective-permute-start | bytes 786440 | tf_op jit(solution)/shard_map/ppermute | solution.py:14
  295.1 6.1 %collective-permute-done.10 = f32[2,2,32,512]{3,2,1,0:T(8,128)S(1)} collective-permute-done((f32[2,2,32,512]{3,2,1,0:T(8,128)S(1)}, f32[2,2,32,512]{3,2,1,0:T(8,128)S(1)}, u32[]{:S(2)}, u32[]{:S(2)}) %collective-permute-start.10) | collective-permute-done | bytes 262176 | tf_op jit(solution)/shard_map/ppermute | solution.py:14
  301.4 2.9 collective-permute-start.11
  304.3 7.2 %collective-permute-done.11 = f32[2,2,32,512]{3,2,1,0:T(8,128)S(1)} collective-permute-done((f32[2,2,32,512]{3,2,1,0:T(8,128)S(1)}, f32[2,2,32,512]{3,2,1,0:T(8,128)S(1)}, u32[]{:S(2)}, u32[]{:S(2)}) %collective-permute-start.11) | collective-permute-done | bytes 262176 | tf_op jit(solution)/shard_map/ppermute | solution.py:14
  311.6 0.3 convolution_bitcast_fusion
  312.0 27.5 %all-reduce.1 = bf16[256,512]{0,1:T(8,128)(2,1)S(1)} all-reduce(f32[256,512]{0,1:T(8,128)S(1)} %convolution_bitcast_fusion), channel_id=1, replica_groups=mesh['context'=64,'tensor'=8] {'tensor'}, use_global_device_ids=true, to_apply=%region_0.1 | all-reduce | flops 131072 | bytes 786432 | tf_op jit(solution)/shard_map/psum | solution.py:121
  339.5 0.8 copy.29
  (76 shorter events, 4.5 us)
Async XLA Ops:
  0.0 19.9 %copy-start = (bf16[3,256,32]{1,2,0:T(8,128)(2,1)S(1)}, bf16[3,256,32]{1,2,0:T(8,128)(2,1)}, u32[]{:S(2)}) copy-start(bf16[3,256,32]{1,2,0:T(8,128)(2,1)} %param.6) | copy-start | bytes 147460
  20.1 0.8 copy-start.1
  21.0 16.8 %collective-permute-start = (f32[2,4,32,512]{3,2,1,0:T(8,128)S(1)}, f32[2,4,32,512]{3,2,1,0:T(8,128)S(1)}, u32[]{:S(2)}, u32[]{:S(2)}) collective-permute-start(f32[2,4,32,512]{3,2,1,0:T(8,128)S(1)} %pad_maximum_fusion), channel_id=1, source_target_pairs={{0,256},{8,264},{16,272},{24,280},{32,288},{40,296},{48,304},{56,3... | collective-permute-start | bytes 1572872 | tf_op jit(solution)/shard_map/ppermute | solution.py:14
  38.1 14.3 %collective-permute-start.1 = (f32[2,4,32,512]{3,2,1,0:T(8,128)S(1)}, f32[2,4,32,512]{3,2,1,0:T(8,128)S(1)}, u32[]{:S(2)}, u32[]{:S(2)}) collective-permute-start(f32[2,4,32,512]{3,2,1,0:T(8,128)S(1)} %maximum_select_fusion), channel_id=1, source_target_pairs={{0,128},{8,136},{16,144},{24,152},{32,160},{40,168},{48,176},{56,1... | collective-permute-start | bytes 1572872 | tf_op jit(solution)/shard_map/ppermute | solution.py:14
  53.1 34.5 %collective-permute-start.2 = (f32[2,4,32,512]{3,2,1,0:T(8,128)S(1)}, f32[2,4,32,512]{3,2,1,0:T(8,128)S(1)}, u32[]{:S(2)}, u32[]{:S(2)}) collective-permute-start(f32[2,4,32,512]{3,2,1,0:T(8,128)S(1)} %maximum_select_fusion.1), channel_id=1, source_target_pairs={{0,64},{8,72},{16,80},{24,88},{32,96},{40,104},{48,112},{56,120},{... | collective-permute-start | bytes 1572872 | tf_op jit(solution)/shard_map/ppermute | solution.py:14
  87.9 67.4 %collective-permute-start.3 = (f32[2,4,32,512]{3,2,1,0:T(8,128)S(1)}, f32[2,4,32,512]{3,2,1,0:T(8,128)S(1)}, u32[]{:S(2)}, u32[]{:S(2)}) collective-permute-start(f32[2,4,32,512]{3,2,1,0:T(8,128)S(1)} %maximum_select_fusion.2), channel_id=1, source_target_pairs={{0,32},{8,40},{16,48},{24,56},{32,0},{40,8},{48,16},{56,24},{64,96... | collective-permute-start | bytes 1572872 | tf_op jit(solution)/shard_map/ppermute | solution.py:14
  155.7 25.6 %collective-permute-start.4 = (f32[2,4,32,512]{3,2,1,0:T(8,128)S(1)}, f32[2,4,32,512]{3,2,1,0:T(8,128)S(1)}, u32[]{:S(2)}, u32[]{:S(2)}) collective-permute-start(f32[2,4,32,512]{3,2,1,0:T(8,128)S(1)} %maximum_select_fusion.3), channel_id=1, source_target_pairs={{0,16},{8,24},{16,0},{24,8},{32,48},{40,56},{48,32},{56,40},{64,80... | collective-permute-start | bytes 1572872 | tf_op jit(solution)/shard_map/ppermute | solution.py:14
  181.6 14.9 %collective-permute-start.5 = (f32[2,4,32,512]{3,2,1,0:T(8,128)S(1)}, f32[2,4,32,512]{3,2,1,0:T(8,128)S(1)}, u32[]{:S(2)}, u32[]{:S(2)}) collective-permute-start(f32[2,4,32,512]{3,2,1,0:T(8,128)S(1)} %maximum_select_fusion.4), channel_id=1, source_target_pairs={{0,8},{8,0},{16,24},{24,16},{32,40},{40,32},{48,56},{56,48},{64,72... | collective-permute-start | bytes 1572872 | tf_op jit(solution)/shard_map/ppermute | solution.py:14
  206.9 8.4 %collective-permute-start.6 = (f32[2,2,32,512]{3,2,1,0:T(8,128)S(1)}, f32[2,2,32,512]{3,2,1,0:T(8,128)S(1)}, u32[]{:S(2)}, u32[]{:S(2)}) collective-permute-start(f32[2,2,32,512]{3,2,1,0:T(8,128)S(1)} %maximum_select_fusion.6), channel_id=1, source_target_pairs={{0,8},{8,0},{16,24},{24,16},{32,40},{40,32},{48,56},{56,48},{64,72... | collective-permute-start | bytes 786440 | tf_op jit(solution)/shard_map/ppermute | solution.py:14
  215.4 16.2 %collective-permute-start.7 = (f32[2,2,32,512]{3,2,1,0:T(8,128)S(1)}, f32[2,2,32,512]{3,2,1,0:T(8,128)S(1)}, u32[]{:S(2)}, u32[]{:S(2)}) collective-permute-start(f32[2,2,32,512]{3,2,1,0:T(8,128)S(1)} %maximum_select_fusion.7), channel_id=1, source_target_pairs={{0,16},{8,24},{16,0},{24,8},{32,48},{40,56},{48,32},{56,40},{64,80... | collective-permute-start | bytes 786440 | tf_op jit(solution)/shard_map/ppermute | solution.py:14
  231.8 28.0 %collective-permute-start.8 = (f32[2,2,32,512]{3,2,1,0:T(8,128)S(1)}, f32[2,2,32,512]{3,2,1,0:T(8,128)S(1)}, u32[]{:S(2)}, u32[]{:S(2)}) collective-permute-start(f32[2,2,32,512]{3,2,1,0:T(8,128)S(1)} %maximum_select_fusion.8), channel_id=1, source_target_pairs={{0,32},{8,40},{16,48},{24,56},{32,0},{40,8},{48,16},{56,24},{64,96... | collective-permute-start | bytes 786440 | tf_op jit(solution)/shard_map/ppermute | solution.py:14
  259.9 30.6 %collective-permute-start.9 = (f32[2,2,32,512]{3,2,1,0:T(8,128)S(1)}, f32[2,2,32,512]{3,2,1,0:T(8,128)S(1)}, u32[]{:S(2)}, u32[]{:S(2)}) collective-permute-start(f32[2,2,32,512]{3,2,1,0:T(8,128)S(1)} %maximum_select_fusion.9), channel_id=1, source_target_pairs={{0,64},{8,72},{16,80},{24,88},{32,96},{40,104},{48,112},{56,120},{... | collective-permute-start | bytes 786440 | tf_op jit(solution)/shard_map/ppermute | solution.py:14
  290.7 10.5 %collective-permute-start.10 = (f32[2,2,32,512]{3,2,1,0:T(8,128)S(1)}, f32[2,2,32,512]{3,2,1,0:T(8,128)S(1)}, u32[]{:S(2)}, u32[]{:S(2)}) collective-permute-start(f32[2,2,32,512]{3,2,1,0:T(8,128)S(1)} %maximum_select_fusion.10), channel_id=1, source_target_pairs={{0,128},{8,136},{16,144},{24,152},{32,160},{40,168},{48,176},{56,1... | collective-permute-start | bytes 786440 | tf_op jit(solution)/shard_map/ppermute | solution.py:14
  301.4 10.3 %copy-start.2 = (bf16[32,256]{1,0:T(8,128)(2,1)S(1)}, bf16[32,256]{1,0:T(8,128)(2,1)}, u32[]{:S(2)}) copy-start(bf16[32,256]{1,0:T(8,128)(2,1)} %param.9) | copy-start | bytes 49156
  301.4 10.3 %copy-start.3 = (f32[32]{0:T(128)S(1)}, f32[32]{0:T(128)}, u32[]{:S(2)}) copy-start(f32[32]{0:T(128)} %param.8) | copy-start | bytes 388
  301.4 10.2 %collective-permute-start.11 = (f32[2,2,32,512]{3,2,1,0:T(8,128)S(1)}, f32[2,2,32,512]{3,2,1,0:T(8,128)S(1)}, u32[]{:S(2)}, u32[]{:S(2)}) collective-permute-start(f32[2,2,32,512]{3,2,1,0:T(8,128)S(1)} %maximum_select_fusion.11), channel_id=1, source_target_pairs={{0,256},{8,264},{16,272},{24,280},{32,288},{40,296},{48,304},{56,3... | collective-permute-start | bytes 786440 | tf_op jit(solution)/shard_map/ppermute | solution.py:14
where the time goes:
time: 343 us; the launch traced here: 340 us
  waiting for transfers between devices  210 us (61%)
  starting transfers between devices  66.2 us (19%)
  blocking collectives  47.3 us (14%)
  matrix products  9.2 us (3%)
  other arithmetic  3.99 us (1%)
    ppermute x12, waiting for transfers between devices, swapped(): return lax.ppermute(value, axis, pairs)  210 us
    ppermute x12, starting transfers between devices, swapped(): return lax.ppermute(value, axis, pairs)  66.2 us
    psum x1, blocking collectives, shards(): mixed_out = lax.psum(partial_terms, 'tensor').astype(jnp.bfloat16)  27.5 us
    all_gather x1, blocking collectives, shards(): lax.all_gather(sequence, 'tensor', axis=0, tiled=True)  19.8 us
  transfers between devices with their start and end apart: 12, of which 12 were waited for; matrix products, arithmetic and copies ran while one was open for 0% of the time, Pallas kernels for 0%

commit v1 on v0

v1 whole, which is shorter than its diff:
```python
import math

import jax
import jax.numpy as jnp
import numpy as np
from jax import lax
from jax.experimental import pallas as pl
from jax.experimental.pallas import tpu as pltpu
from jax.sharding import PartitionSpec as P

ROWS = 256
LANES = 128
LENGTH = ROWS * LANES
PIECE = 4
RANKS = ROWS // PIECE


def split_table(table):
    upper = table.astype(jnp.bfloat16)
    lower = (table - upper.astype(np.float64)).astype(jnp.bfloat16)
    return upper, lower


def tables():
    slot = np.arange(ROWS)
    row = (slot % RANKS) * PIECE + slot // RANKS
    low = np.arange(ROWS)
    lane = np.arange(LANES)
    turn = 2.0 * np.pi * np.outer(low + 0.25, row) / ROWS
    outer = np.concatenate([np.cos(turn), -np.sin(turn)], axis=0)
    turn = 2.0 * np.pi * np.outer(low + 0.25, lane) / LENGTH
    twist = np.stack([np.cos(turn), np.sin(turn)]).astype(np.float32)
    turn = 2.0 * np.pi * (np.outer(lane, lane) % LANES) / LANES
    cos_part, sin_part = np.cos(turn), np.sin(turn)
    inner = np.block([[cos_part, -sin_part], [sin_part, cos_part]])
    return (
        *split_table(outer),
        *split_table(outer.T / LENGTH),
        *split_table(inner),
        *split_table(inner.T),
        twist,
    )


def dot(left, right):
    return jnp.dot(left, right, preferred_element_type=jnp.float32)


def split_value(value):
    upper = value.astype(jnp.bfloat16)
    lower = (value - upper.astype(jnp.float32)).astype(jnp.bfloat16)
    return upper, lower


def project_kernel(gathered_ref, proj_ref, filter_ref, send_ref, gated_ref, gate_ref, rows_ref):
    width = gathered_ref.shape[0]
    tok_len = filter_ref.shape[1]
    channels = filter_ref.shape[0]
    sequence = gathered_ref[:, :tok_len]
    first, gate, value = [
        lax.dot_general(
            proj_ref[index], sequence, (((0,), (0,)), ((), ())), preferred_element_type=jnp.float32
        )
        for index in range(3)
    ]
    gated = value * first
    gated_ref[...] = gated
    gate_ref[...] = gate
    for piece in range(PIECE):
        cut = slice(piece * LANES, (piece + 1) * LANES)
        for half in range(2):
            span = slice(half * channels, (half + 1) * channels)
            rows_ref[span, piece, :] = gated[:, cut]
            rows_ref[span, PIECE + piece, :] = filter_ref[:, cut]
    send_ref[...] = rows_ref[...].astype(jnp.bfloat16)


def convolve_kernel(
    half_ref, recv_ref, fwd_hi, fwd_lo, back_hi, back_lo, in_hi, in_lo, out_hi, out_lo, twist_ref,
    send_ref, rows_ref, result_ref,
):
    rows_ref[...] = recv_ref[...].astype(jnp.float32)
    both = jnp.concatenate(
        [
            jnp.concatenate([rows_ref[:, piece, :], rows_ref[:, PIECE + piece, :]], axis=1)
            for piece in range(PIECE)
        ],
        axis=0,
    ).astype(jnp.bfloat16)
    cos_part = twist_ref[0]
    sin_part = twist_ref[1]
    outer = dot(fwd_hi[...], both) + dot(fwd_lo[...], both)
    real, imag = outer[:ROWS], outer[ROWS:]
    turned = []
    for cut in (slice(0, LANES), slice(LANES, 2 * LANES)):
        turned.append(
            jnp.concatenate(
                [
                    real[:, cut] * cos_part + imag[:, cut] * sin_part,
                    imag[:, cut] * cos_part - real[:, cut] * sin_part,
                ],
                axis=1,
            )
        )
    upper, lower = split_value(jnp.concatenate(turned, axis=0))
    spectra = dot(upper, in_hi[...]) + dot(lower, in_hi[...]) + dot(upper, in_lo[...])
    source_real, source_imag = spectra[:ROWS, :LANES], spectra[:ROWS, LANES:]
    filter_real, filter_imag = spectra[ROWS:, :LANES], spectra[ROWS:, LANES:]
    product = jnp.concatenate(
        [
            source_real * filter_real - source_imag * filter_imag,
            source_real * filter_imag + source_imag * filter_real,
        ],
        axis=1,
    )
    upper, lower = split_value(product)
    inner = dot(upper, out_hi[...]) + dot(lower, out_hi[...]) + dot(upper, out_lo[...])
    real, imag = inner[:, :LANES], inner[:, LANES:]
    upper, lower = split_value(
        jnp.concatenate(
            [real * cos_part - imag * sin_part, imag * cos_part + real * sin_part], axis=0
        )
    )
    span = pl.ds(pl.multiple_of(half_ref[0] * (ROWS // 2), ROWS // 2), ROWS // 2)
    left_hi, left_lo = back_hi[span, :], back_lo[span, :]
    result = dot(left_hi, upper) + dot(left_hi, lower) + dot(left_lo, upper)
    for piece in range(PIECE // 2):
        result_ref[:, piece, :] = result[piece * RANKS : (piece + 1) * RANKS]
    send_ref[...] = result_ref[...].astype(jnp.bfloat16)


def gate_kernel(recv_ref, gated_ref, gate_ref, skip_ref, send_ref, rows_ref):
    channels = gated_ref.shape[0]
    rows_ref[...] = recv_ref[...].astype(jnp.float32)
    convolved = jnp.concatenate(
        [
            rows_ref[half * channels : (half + 1) * channels, piece, :]
            for half in range(2)
            for piece in range(PIECE // 2)
        ],
        axis=1,
    )
    convolved = convolved + skip_ref[...] * gated_ref[...]
    out_gated = (convolved * gate_ref[...]).astype(jnp.bfloat16)
    for copy in range(send_ref.shape[0]):
        send_ref[copy] = out_gated


def whole(count):
    return [pl.BlockSpec(memory_space=pltpu.VMEM) for _ in range(count)]


def shards(sequence, proj_in, conv_filter, skip_gain, proj_out):
    channels, tok_len = sequence.shape
    width = proj_out.shape[1]
    groups = lax.axis_size("tensor")
    ranks = lax.axis_size("context")
    rank = lax.axis_index("context")
    half = (rank // (ranks // 2)).astype(jnp.int32).reshape(1)

    packed = jnp.concatenate([sequence, proj_out], axis=1)
    gathered = lax.all_to_all(
        jnp.broadcast_to(packed[None], (groups, *packed.shape)), "tensor", 0, 0, tiled=True
    ).reshape(width, tok_len + width)

    send, gated, gate = pl.pallas_call(
        project_kernel,
        out_shape=(
            jax.ShapeDtypeStruct((ranks, 2 * PIECE, LANES), jnp.bfloat16),
            jax.ShapeDtypeStruct((channels, tok_len), jnp.float32),
            jax.ShapeDtypeStruct((channels, tok_len), jnp.float32),
        ),
        in_specs=whole(3),
        out_specs=tuple(whole(3)),
        scratch_shapes=[pltpu.VMEM((ranks, 2 * PIECE, LANES), jnp.float32)],
        compiler_params=pltpu.CompilerParams(vmem_limit_bytes=16 * 2**20),
        name="project",
    )(gathered, proj_in, conv_filter)

    recv = lax.all_to_all(send, "context", 0, 0, tiled=True)

    constants = [jnp.asarray(table) for table in tables()]
    send = pl.pallas_call(
        convolve_kernel,
        out_shape=jax.ShapeDtypeStruct((ranks, PIECE // 2, LANES), jnp.bfloat16),
        in_specs=[pl.BlockSpec(memory_space=pltpu.SMEM)] + whole(1 + len(constants)),
        out_specs=whole(1)[0],
        scratch_shapes=[
            pltpu.VMEM((ranks, 2 * PIECE, LANES), jnp.float32),
            pltpu.VMEM((ranks, PIECE // 2, LANES), jnp.float32),
        ],
        compiler_params=pltpu.CompilerParams(vmem_limit_bytes=24 * 2**20),
        name="convolve",
    )(half, recv, *constants)

    recv = lax.all_to_all(send, "context", 0, 0, tiled=True)

    send = pl.pallas_call(
        gate_kernel,
        out_shape=jax.ShapeDtypeStruct((groups, channels, tok_len), jnp.bfloat16),
        in_specs=whole(4),
        out_specs=whole(1)[0],
        scratch_shapes=[pltpu.VMEM((ranks, PIECE // 2, LANES), jnp.float32)],
        compiler_params=pltpu.CompilerParams(vmem_limit_bytes=16 * 2**20),
        name="gate",
    )(recv, gated, gate, skip_gain.reshape(channels, 1))

    out_gated = lax.all_to_all(send, "tensor", 0, 0, tiled=True).reshape(width, tok_len)
    mixed = lax.dot_general(
        gathered[:, tok_len:],
        out_gated,
        (((0,), (0,)), ((), ())),
        preferred_element_type=jnp.float32,
    )
    return mixed.astype(jnp.bfloat16)


def solution(mesh):
    return jax.shard_map(
        shards,
        mesh=mesh,
        in_specs=(
            P("tensor", "context"),
            P(None, None, "tensor"),
            P("tensor", "context"),
            P("tensor"),
            P("tensor", None),
        ),
        out_specs=P(None, "context"),
        check_vma=False,
    )
```

time: 343 us -> 85.1 us (0.25)
  waiting for transfers between devices: 210 us -> 34.4 us
  blocking collectives: 47.3 us -> 11.4 us
  starting transfers between devices: 66.2 us -> 31.9 us
  matrix products: 9.2 us -> 0.95 us
    ppermute x12 -> x0, waiting for transfers between devices: 210 us -> none  [swapped(): return lax.ppermute(value, axis, pairs)]
    ppermute x12 -> x0, starting transfers between devices: 66.2 us -> none  [swapped(): return lax.ppermute(value, axis, pairs)]
    all_to_all x0 -> x3, waiting for transfers between devices: none -> 34.4 us  [the longest x2 26.5 us: shards(): recv = lax.all_to_all(send, 'context', 0, 0, tiled=True)]
    all_to_all x0 -> x3, starting transfers between devices: none -> 31.9 us  [the longest x2 21.6 us: shards(): recv = lax.all_to_all(send, 'context', 0, 0, tiled=True)]
    psum x1 -> x0, blocking collectives: 27.5 us -> none  [shards(): mixed_out = lax.psum(partial_terms, 'tensor').astype(jnp.bfloat16)]
    all_gather x1 -> x0, blocking collectives: 19.8 us -> none  [shards(): lax.all_gather(sequence, 'tensor', axis=0, tiled=True)]
    all_to_all x0 -> x1, blocking collectives: none -> 11.4 us  [shards(): lax.all_to_all(send, 'tensor', 0, 0, tiled=True).reshape(width, tok_len)]
    dot_general x18 -> x1, matrix products: 9.2 us -> 0.95 us  [shards(): lax.dot_general(gathered[:, tok_len:], out_gated, (((0,), (0,)), ((), ())...]
  transfers between devices with their start and end apart: 12 -> 3, of which waited for: 12 -> 3; matrix products, arithmetic and copies ran while one was open for 0% -> 0% of each run, Pallas kernels for 0% -> 0%
where the time goes in v1:
time: 85.1 us; the launch traced here: 84.7 us
  waiting for transfers between devices  34.4 us (40%)
  starting transfers between devices  31.9 us (37%)
  blocking collectives  11.4 us (13%)
  Pallas kernels  3.31 us (4%)
  local copies, waits for them, and re-layouts  1.73 us (2%)
  matrix products  0.95 us (1%)
    all_to_all x2, waiting for transfers between devices, shards(): recv = lax.all_to_all(send, 'context', 0, 0, tiled=True)  26.5 us
    all_to_all x2, starting transfers between devices, shards(): recv = lax.all_to_all(send, 'context', 0, 0, tiled=True)  21.6 us
    all_to_all x1, blocking collectives, shards(): lax.all_to_all(send, 'tensor', 0, 0, tiled=True).reshape(width, tok_len)  11.4 us
    all_to_all x1, starting transfers between devices, shards(): lax.all_to_all(jnp.broadcast_to(packed[None], (groups, *packed.shape)), '...  10.4 us
    all_to_all x1, waiting for transfers between devices, shards(): lax.all_to_all(jnp.broadcast_to(packed[None], (groups, *packed.shape)), '...  7.93 us
    pallas_call x1, Pallas kernels, shards(): pl.pallas_call(convolve_kernel, out_shape=jax.ShapeDtypeStruct((ranks, PI...  2.2 us
  transfers between devices with their start and end apart: 3, of which 3 were waited for; matrix products, arithmetic and copies ran while one was open for 0% of the time, Pallas kernels for 0%

profile of v1, /device:TPU:1, one launch (start us, length us, event | category | flops | bytes accessed | tf_op | source)
XLA Modules:
  0.0 84.7 jit_solution(16099874541533069170)
XLA Ops:
  0.0 0.8 pad_maximum_fusion
  0.8 0.8 broadcast_in_dim.2
  1.6 0.0 copy-start.10
  1.6 0.0 copy-start.9
  1.6 0.0 copy-start.4
  1.6 0.0 copy-start.6
  1.6 0.0 copy-start.7
  1.6 0.0 copy-start.8
  1.6 10.4 %all-to-all-start = ((bf16[8,32,768]{2,1,0:T(8,128)(2,1)}), bf16[8,32,768]{2,1,0:T(8,128)(2,1)S(1)}, u32[]{:S(2)}, u32[]{:S(2)}) async-start(bf16[8,32,768]{2,1,0:T(8,128)(2,1)} %broadcast_in_dim.2), calls=%async_computation | async-start | bytes 786432 | tf_op jit(solution)/shard_map/all_to_all | solution.py:162
  12.0 0.0 copy-done.10
  12.0 0.0 copy-start.3
  12.0 0.2 copy.15.proj_ref
  12.1 7.9 %all-to-all-done = bf16[8,32,768]{2,1,0:T(8,128)(2,1)S(1)} async-done(((bf16[8,32,768]{2,1,0:T(8,128)(2,1)}), bf16[8,32,768]{2,1,0:T(8,128)(2,1)S(1)}, u32[]{:S(2)}, u32[]{:S(2)}) %all-to-all-start) | async-done | bytes 393248 | tf_op jit(solution)/shard_map/all_to_all | solution.py:162
  20.1 0.0 copy-done.9
  20.1 0.0 copy-start.1
  20.1 0.0 copy-start.2
  20.1 0.0 copy-start.5
  20.1 1.0 %project.1 = (bf16[64,8,128]{2,1,0:T(8,128)(2,1)}, f32[32,512]{1,0:T(8,128)S(1)}, f32[32,512]{1,0:T(8,128)S(1)}) custom-call(bf16[256,768]{1,0:T(8,128)(2,1)S(1)} %bitcast.5, bf16[3,256,32]{2,1,0:T(8,128)(2,1)S(1)} %copy.15.proj_ref, f32[32,512]{1,0:T(8,128)S(1)} %copy-done.9), custom_call_target="tpu_custom_call" | custom-call | tf_op jit(solution)/shard_map/project/pallas_call | solution.py:166
  21.1 0.0 copy-start
  21.1 14.1 %all-to-all-start.1 = ((bf16[64,8,128]{2,1,0:T(8,128)(2,1)}), bf16[64,8,128]{2,1,0:T(8,128)(2,1)S(1)}, u32[]{:S(2)}, u32[]{:S(2)}) async-start(bf16[64,8,128]{2,1,0:T(8,128)(2,1)} %get-tuple-element.8), calls=%async_computation.1 | async-start | bytes 262144 | tf_op jit(solution)/shard_map/all_to_all | solution.py:180
  35.3 14.0 %all-to-all-done.1.recv_ref = bf16[64,8,128]{2,1,0:T(8,128)(2,1)S(1)} async-done(((bf16[64,8,128]{2,1,0:T(8,128)(2,1)}), bf16[64,8,128]{2,1,0:T(8,128)(2,1)S(1)}, u32[]{:S(2)}, u32[]{:S(2)}) %all-to-all-start.1) | async-done | bytes 131104 | tf_op jit(solution)/shard_map/all_to_all | solution.py:180
  49.3 0.0 copy-done.4
  49.3 0.0 copy-done.6
  49.3 0.0 copy-done.7
  49.3 0.0 copy-done.8
  49.3 0.0 copy-done.3
  49.3 0.0 copy-done.1
  49.3 0.0 copy-done.2
  49.3 0.0 copy-done.5
  49.4 0.0 copy-done
  49.4 2.2 %convolve.1 = bf16[64,2,128]{2,1,0:T(2,128)(2,1)} custom-call(s32[1]{0:T(128)} %bitcast.1.half_ref, bf16[64,8,128]{2,1,0:T(8,128)(2,1)S(1)} %all-to-all-done.1.recv_ref, bf16[512,256]{1,0:T(8,128)(2,1)S(1)} %copy-done, bf16[512,256]{1,0:T(8,128)(2,1)S(1)} %copy-done.1, bf16[256,512]{1,0:T(8,128)(2,1)S(1)} %copy-done.2, bf16[256,512]{1,0:T(8,128)(2,1)S(1)} %copy-done.3, ...), custom_call_target="tpu_custom_call" | custom-call | tf_op jit(solution)/shard_map/convolve/pallas_call | solution.py:183
  51.6 7.4 %all-to-all-start.2 = ((bf16[64,2,128]{2,1,0:T(2,128)(2,1)}), bf16[64,2,128]{2,1,0:T(2,128)(2,1)S(1)}, u32[]{:S(2)}, u32[]{:S(2)}) async-start(bf16[64,2,128]{2,1,0:T(2,128)(2,1)} %convolve.1), calls=%async_computation.2 | async-start | bytes 65536 | tf_op jit(solution)/shard_map/all_to_all | solution.py:196
  59.0 0.0 copy-start.11
  59.0 0.6 copy-done.11
  59.7 0.1 copy.16.skip_ref
  59.8 12.5 %all-to-all-done.2.recv_ref = bf16[64,2,128]{2,1,0:T(2,128)(2,1)S(1)} async-done(((bf16[64,2,128]{2,1,0:T(2,128)(2,1)}), bf16[64,2,128]{2,1,0:T(2,128)(2,1)S(1)}, u32[]{:S(2)}, u32[]{:S(2)}) %all-to-all-start.2) | async-done | bytes 32800 | tf_op jit(solution)/shard_map/all_to_all | solution.py:196
  72.2 0.1 gate.1
  72.3 11.4 %all_to_all.20 = bf16[8,32,512]{2,1,0:T(8,128)(2,1)S(1)} all-to-all(bf16[8,32,512]{2,1,0:T(8,128)(2,1)S(1)} %gate.1), channel_id=1, replica_groups=mesh['context'=64,'tensor'=8] {'tensor'}, dimensions={0} | all-to-all | bytes 524288 | tf_op jit(solution)/shard_map/all_to_all | solution.py:208
  83.7 1.0 %convolution_convert_fusion = bf16[256,512]{1,0:T(8,128)(2,1)} fusion(bf16[256,512]{1,0:T(8,128)(2,1)S(1)} %bitcast.7, bf16[256,768]{1,0:T(8,128)(2,1)S(1)} %bitcast.6), kind=kOutput, calls=%fused_computation | convolution fusion | flops 67239936 | bytes 655360 | tf_op jit(solution)/shard_map/dot_general | solution.py:209
Async XLA Ops:
  1.6 10.4 %copy-start.10 = (bf16[3,256,32]{1,2,0:T(8,128)(2,1)S(1)}, bf16[3,256,32]{1,2,0:T(8,128)(2,1)}, u32[]{:S(2)}) copy-start(bf16[3,256,32]{1,2,0:T(8,128)(2,1)} %param.15) | copy-start | bytes 147460
  1.6 18.5 %copy-start.9 = (f32[32,512]{1,0:T(8,128)S(1)}, f32[32,512]{1,0:T(8,128)}, u32[]{:S(2)}) copy-start(f32[32,512]{1,0:T(8,128)} %filter_ref.1) | copy-start | bytes 196612
  1.6 47.7 %copy-start.4 = (f32[2,256,128]{2,1,0:T(8,128)S(1)}, f32[2,256,128]{2,1,0:T(8,128)}, u32[]{:S(2)}) copy-start(f32[2,256,128]{2,1,0:T(8,128)} %constant.48.clone.twist_ref) | copy-start | bytes 786436
  1.6 47.7 %copy-start.6 = (bf16[256,256]{1,0:T(8,128)(2,1)S(1)}, bf16[256,256]{1,0:T(8,128)(2,1)}, u32[]{:S(2)}) copy-start(bf16[256,256]{1,0:T(8,128)(2,1)} %constant.45.clone.in_lo) | copy-start | bytes 393220
  1.6 47.7 %copy-start.7 = (bf16[256,256]{1,0:T(8,128)(2,1)S(1)}, bf16[256,256]{1,0:T(8,128)(2,1)}, u32[]{:S(2)}) copy-start(bf16[256,256]{1,0:T(8,128)(2,1)} %constant.46.clone.out_hi) | copy-start | bytes 393220
  1.6 47.7 %copy-start.8 = (bf16[256,256]{1,0:T(8,128)(2,1)S(1)}, bf16[256,256]{1,0:T(8,128)(2,1)}, u32[]{:S(2)}) copy-start(bf16[256,256]{1,0:T(8,128)(2,1)} %constant.47.clone.out_lo) | copy-start | bytes 393220
  1.6 18.5 %all-to-all-start = ((bf16[8,32,768]{2,1,0:T(8,128)(2,1)}), bf16[8,32,768]{2,1,0:T(8,128)(2,1)S(1)}, u32[]{:S(2)}, u32[]{:S(2)}) async-start(bf16[8,32,768]{2,1,0:T(8,128)(2,1)} %broadcast_in_dim.2), calls=%async_computation | async-start | bytes 786432 | tf_op jit(solution)/shard_map/all_to_all | solution.py:162
  12.0 37.3 %copy-start.3 = (bf16[256,512]{1,0:T(8,128)(2,1)S(1)}, bf16[256,512]{1,0:T(8,128)(2,1)}, u32[]{:S(2)}) copy-start(bf16[256,512]{1,0:T(8,128)(2,1)} %constant.43.clone.back_lo) | copy-start | bytes 786436
  20.1 29.3 %copy-start.1 = (bf16[512,256]{1,0:T(8,128)(2,1)S(1)}, bf16[512,256]{1,0:T(8,128)(2,1)}, u32[]{:S(2)}) copy-start(bf16[512,256]{1,0:T(8,128)(2,1)} %constant.41.clone.fwd_lo) | copy-start | bytes 786436
  20.1 29.3 %copy-start.2 = (bf16[256,512]{1,0:T(8,128)(2,1)S(1)}, bf16[256,512]{1,0:T(8,128)(2,1)}, u32[]{:S(2)}) copy-start(bf16[256,512]{1,0:T(8,128)(2,1)} %constant.42.clone.back_hi) | copy-start | bytes 786436
  20.1 29.3 %copy-start.5 = (bf16[256,256]{1,0:T(8,128)(2,1)S(1)}, bf16[256,256]{1,0:T(8,128)(2,1)}, u32[]{:S(2)}) copy-start(bf16[256,256]{1,0:T(8,128)(2,1)} %constant.44.clone.in_hi) | copy-start | bytes 393220
  21.1 28.3 %copy-start = (bf16[512,256]{1,0:T(8,128)(2,1)S(1)}, bf16[512,256]{1,0:T(8,128)(2,1)}, u32[]{:S(2)}) copy-start(bf16[512,256]{1,0:T(8,128)(2,1)} %constant.40.clone.fwd_hi) | copy-start | bytes 786436
  21.1 28.2 %all-to-all-start.1 = ((bf16[64,8,128]{2,1,0:T(8,128)(2,1)}), bf16[64,8,128]{2,1,0:T(8,128)(2,1)S(1)}, u32[]{:S(2)}, u32[]{:S(2)}) async-start(bf16[64,8,128]{2,1,0:T(8,128)(2,1)} %get-tuple-element.8), calls=%async_computation.1 | async-start | bytes 262144 | tf_op jit(solution)/shard_map/all_to_all | solution.py:180
  51.6 20.7 %all-to-all-start.2 = ((bf16[64,2,128]{2,1,0:T(2,128)(2,1)}), bf16[64,2,128]{2,1,0:T(2,128)(2,1)S(1)}, u32[]{:S(2)}, u32[]{:S(2)}) async-start(bf16[64,2,128]{2,1,0:T(2,128)(2,1)} %convolve.1), calls=%async_computation.2 | async-start | bytes 65536 | tf_op jit(solution)/shard_map/all_to_all | solution.py:196
  59.0 0.7 copy-start.11

commit v2 on v1

--- a/solution.py
+++ b/solution.py
@@ -13,6 +13,15 @@
 LENGTH = ROWS * LANES
 PIECE = 4
 RANKS = ROWS // PIECE
+LINES, RING = 4, 16
+CHANNELS = RANKS // 2
+
+TURN = 2
+HALVES = [
+    [(outer + TURN) % LINES * RING + inner for outer in range(LINES) for inner in ring]
+    for ring in (range(RING // 2, RING), range(RING // 2 - 1, -1, -1))
+]
+ORDER = HALVES[0] + HALVES[1]
 
 
 def split_table(table):
@@ -22,20 +31,25 @@
 
 
 def tables():
-    slot = np.arange(ROWS)
-    row = (slot % RANKS) * PIECE + slot // RANKS
+    come = np.concatenate([np.asarray(ORDER) * PIECE + piece for piece in range(PIECE)])
+    go = np.concatenate(
+        [np.asarray(half) * PIECE + piece for half in HALVES for piece in range(PIECE)]
+    )
     low = np.arange(ROWS)
     lane = np.arange(LANES)
-    turn = 2.0 * np.pi * np.outer(low + 0.25, row) / ROWS
-    outer = np.concatenate([np.cos(turn), -np.sin(turn)], axis=0)
+
+    def outer(row):
+        turn = 2.0 * np.pi * np.outer(low + 0.25, row) / ROWS
+        return np.concatenate([np.cos(turn), -np.sin(turn)], axis=0)
+
     turn = 2.0 * np.pi * np.outer(low + 0.25, lane) / LENGTH
     twist = np.stack([np.cos(turn), np.sin(turn)]).astype(np.float32)
     turn = 2.0 * np.pi * (np.outer(lane, lane) % LANES) / LANES
     cos_part, sin_part = np.cos(turn), np.sin(turn)
     inner = np.block([[cos_part, -sin_part], [sin_part, cos_part]])
     return (
-        *split_table(outer),
-        *split_table(outer.T / LENGTH),
+        *split_table(outer(come)),
+        *split_table(outer(go).T / LENGTH),
         *split_table(inner),
         *split_table(inner.T),
         twist,
@@ -52,10 +66,17 @@
     return upper, lower
 
 
-def project_kernel(gathered_ref, proj_ref, filter_ref, send_ref, gated_ref, gate_ref, rows_ref):
-    width = gathered_ref.shape[0]
-    tok_len = filter_ref.shape[1]
-    channels = filter_ref.shape[0]
+def spread_kernel(sequence_ref, proj_ref, send_ref):
+    tok_len = sequence_ref.shape[1]
+    for copy in range(send_ref.shape[0]):
+        send_ref[copy, :, :tok_len] = sequence_ref[...]
+        send_ref[copy, :, tok_len:] = proj_ref[...]
+
+
+def project_kernel(
+    gathered_ref, proj_ref, filter_ref, skip_ref, send_ref, gate_ref, direct_ref, rows_ref
+):
+    channels, tok_len = filter_ref.shape
     sequence = gathered_ref[:, :tok_len]
     first, gate, value = [
         lax.dot_general(
@@ -64,8 +85,8 @@
         for index in range(3)
     ]
     gated = value * first
-    gated_ref[...] = gated
     gate_ref[...] = gate
+    direct_ref[...] = skip_ref[...] * gated
     for piece in range(PIECE):
         cut = slice(piece * LANES, (piece + 1) * LANES)
         for half in range(2):
@@ -124,24 +145,15 @@
     span = pl.ds(pl.multiple_of(half_ref[0] * (ROWS // 2), ROWS // 2), ROWS // 2)
     left_hi, left_lo = back_hi[span, :], back_lo[span, :]
     result = dot(left_hi, upper) + dot(left_hi, lower) + dot(left_lo, upper)
-    for piece in range(PIECE // 2):
-        result_ref[:, piece, :] = result[piece * RANKS : (piece + 1) * RANKS]
+    for piece in range(PIECE):
+        result_ref[:, piece, :] = result[piece * CHANNELS : (piece + 1) * CHANNELS]
     send_ref[...] = result_ref[...].astype(jnp.bfloat16)
 
 
-def gate_kernel(recv_ref, gated_ref, gate_ref, skip_ref, send_ref, rows_ref):
-    channels = gated_ref.shape[0]
+def gate_kernel(recv_ref, gate_ref, direct_ref, send_ref, rows_ref):
     rows_ref[...] = recv_ref[...].astype(jnp.float32)
-    convolved = jnp.concatenate(
-        [
-            rows_ref[half * channels : (half + 1) * channels, piece, :]
-            for half in range(2)
-            for piece in range(PIECE // 2)
-        ],
-        axis=1,
-    )
-    convolved = convolved + skip_ref[...] * gated_ref[...]
-    out_gated = (convolved * gate_ref[...]).astype(jnp.bfloat16)
+    convolved = jnp.concatenate([rows_ref[:, piece, :] for piece in range(PIECE)], axis=1)
+    out_gated = ((convolved + direct_ref[...]) * gate_ref[...]).astype(jnp.bfloat16)
     for copy in range(send_ref.shape[0]):
         send_ref[copy] = out_gated
 
@@ -155,55 +167,59 @@
     width = proj_out.shape[1]
     groups = lax.axis_size("tensor")
     ranks = lax.axis_size("context")
-    rank = lax.axis_index("context")
-    half = (rank // (ranks // 2)).astype(jnp.int32).reshape(1)
-
-    packed = jnp.concatenate([sequence, proj_out], axis=1)
-    gathered = lax.all_to_all(
-        jnp.broadcast_to(packed[None], (groups, *packed.shape)), "tensor", 0, 0, tiled=True
-    ).reshape(width, tok_len + width)
-
-    send, gated, gate = pl.pallas_call(
+    half = (1 - lax.axis_index("context") % RING // (RING // 2)).astype(jnp.int32).reshape(1)
+
+    send = pl.pallas_call(
+        spread_kernel,
+        out_shape=pltpu.VMEM((groups, channels, tok_len + width), jnp.bfloat16),
+        in_specs=whole(2),
+        out_specs=whole(1)[0],
+        name="spread",
+    )(sequence, proj_out)
+
+    gathered = lax.all_to_all(send, "tensor", 0, 0, tiled=True).reshape(width, tok_len + width)
+
+    send, gate, direct = pl.pallas_call(
         project_kernel,
         out_shape=(
-            jax.ShapeDtypeStruct((ranks, 2 * PIECE, LANES), jnp.bfloat16),
-            jax.ShapeDtypeStruct((channels, tok_len), jnp.float32),
-            jax.ShapeDtypeStruct((channels, tok_len), jnp.float32),
+            pltpu.VMEM((ranks, 2 * PIECE, LANES), jnp.bfloat16),
+            pltpu.VMEM((channels, tok_len), jnp.float32),
+            pltpu.VMEM((channels, tok_len), jnp.float32),
         ),
-        in_specs=whole(3),
+        in_specs=whole(4),
         out_specs=tuple(whole(3)),
         scratch_shapes=[pltpu.VMEM((ranks, 2 * PIECE, LANES), jnp.float32)],
         compiler_params=pltpu.CompilerParams(vmem_limit_bytes=16 * 2**20),
         name="project",
-    )(gathered, proj_in, conv_filter)
-
-    recv = lax.all_to_all(send, "context", 0, 0, tiled=True)
+    )(gathered, proj_in, conv_filter, skip_gain.reshape(channels, 1))
+
+    recv = lax.all_to_all(send, "context", 0, 0, axis_index_groups=[ORDER], tiled=True)
 
     constants = [jnp.asarray(table) for table in tables()]
     send = pl.pallas_call(
         convolve_kernel,
-        out_shape=jax.ShapeDtypeStruct((ranks, PIECE // 2, LANES), jnp.bfloat16),
+        out_shape=pltpu.VMEM((channels, PIECE, LANES), jnp.bfloat16),
         in_specs=[pl.BlockSpec(memory_space=pltpu.SMEM)] + whole(1 + len(constants)),
         out_specs=whole(1)[0],
         scratch_shapes=[
             pltpu.VMEM((ranks, 2 * PIECE, LANES), jnp.float32),
-            pltpu.VMEM((ranks, PIECE // 2, LANES), jnp.float32),
+            pltpu.VMEM((channels, PIECE, LANES), jnp.float32),
         ],
         compiler_params=pltpu.CompilerParams(vmem_limit_bytes=24 * 2**20),
         name="convolve",
     )(half, recv, *constants)
 
-    recv = lax.all_to_all(send, "context", 0, 0, tiled=True)
+    recv = lax.all_to_all(send, "context", 0, 0, axis_index_groups=HALVES, tiled=True)
 
     send = pl.pallas_call(
         gate_kernel,
-        out_shape=jax.ShapeDtypeStruct((groups, channels, tok_len), jnp.bfloat16),
-        in_specs=whole(4),
+        out_shape=pltpu.VMEM((groups, channels, tok_len), jnp.bfloat16),
+        in_specs=whole(3),
         out_specs=whole(1)[0],
-        scratch_shapes=[pltpu.VMEM((ranks, PIECE // 2, LANES), jnp.float32)],
+        scratch_shapes=[pltpu.VMEM((channels, PIECE, LANES), jnp.float32)],
         compiler_params=pltpu.CompilerParams(vmem_limit_bytes=16 * 2**20),
         name="gate",
-    )(recv, gated, gate, skip_gain.reshape(channels, 1))
+    )(recv, gate, direct)
 
     out_gated = lax.all_to_all(send, "tensor", 0, 0, tiled=True).reshape(width, tok_len)
     mixed = lax.dot_general(

time: 85.1 us -> 74.1 us (0.87)
  waiting for transfers between devices: 34.4 us -> 13.9 us
  blocking collectives: 11.4 us -> 25.8 us
  starting transfers between devices: 31.9 us -> 28.4 us
  local copies, waits for them, and re-layouts: 1.73 us -> 0.3 us
  Pallas kernels: 3.31 us -> 4.2 us
    all_to_all x3 -> x2, waiting for transfers between devices: 34.4 us -> 13.9 us  [the longest x1 7.83 us: shards(): lax.all_to_all(send, 'tensor', 0, 0, tiled=True)]
    all_to_all x0 -> x1, blocking collectives: none -> 14.2 us  [shards(): lax.all_to_all(send, 'context', 0, 0, axis_index_groups=HALVES, tiled=True)]
    all_to_all x3 -> x2, starting transfers between devices: 31.9 us -> 28.4 us  [the longest x1 18 us: shards(): lax.all_to_all(send, 'context', 0, 0, axis_index_groups=[ORDER], tiled=True)]
    pallas_call x3 -> x4, Pallas kernels: 3.31 us -> 4.2 us  [the longest x1 1.57 us: shards(): pl.pallas_call(convolve_kernel, out_shape=pltpu.VMEM((channels, PIECE, LA...]
  transfers between devices with their start and end apart: 3 -> 2, of which waited for: 3 -> 2; matrix products, arithmetic and copies ran while one was open for 0% -> 0% of each run, Pallas kernels for 0% -> 0%
where the time goes in v2:
time: 74.1 us; the launch traced here: 73.7 us
  starting transfers between devices  28.4 us (38%)
  blocking collectives  25.8 us (35%)
  waiting for transfers between devices  13.9 us (19%)
  Pallas kernels  4.2 us (6%)
  matrix products  0.95 us (1%)
    all_to_all x1, starting transfers between devices, shards(): lax.all_to_all(send, 'context', 0, 0, axis_index_groups=[ORDER], tiled=True)  18 us
    all_to_all x1, blocking collectives, shards(): lax.all_to_all(send, 'context', 0, 0, axis_index_groups=HALVES, tiled=True)  14.2 us
    all_to_all x1, blocking collectives, shards(): lax.all_to_all(send, 'tensor', 0, 0, tiled=True).reshape(width, tok_len)  11.6 us
    all_to_all x1, starting transfers between devices, shards(): lax.all_to_all(send, 'tensor', 0, 0, tiled=True)  10.4 us
    all_to_all x1, waiting for transfers between devices, shards(): lax.all_to_all(send, 'tensor', 0, 0, tiled=True)  7.83 us
    all_to_all x1, waiting for transfers between devices, shards(): lax.all_to_all(send, 'context', 0, 0, axis_index_groups=[ORDER], tiled=True)  6.05 us
    pallas_call x1, Pallas kernels, shards(): pl.pallas_call(convolve_kernel, out_shape=pltpu.VMEM((channels, PIECE, LA...  1.57 us
    pallas_call x1, Pallas kernels, shards(): pl.pallas_call(spread_kernel, out_shape=pltpu.VMEM((groups, channels, tok...  1.55 us
  transfers between devices with their start and end apart: 2, of which 2 were waited for; matrix products, arithmetic and copies ran while one was open for 0% of the time, Pallas kernels for 0%

profile of v2, /device:TPU:1, one launch (start us, length us, event | category | flops | bytes accessed | tf_op | source)
XLA Modules:
  0.0 73.7 jit_solution(13761013421206876917)
XLA Ops:
  0.0 1.5 %spread.1 = bf16[8,32,768]{2,1,0:T(8,128)(2,1)} custom-call(bf16[32,512]{1,0:T(8,128)(2,1)} %sequence_ref.1, bf16[32,256]{1,0:T(8,128)(2,1)} %proj_ref.2), custom_call_target="tpu_custom_call" | custom-call | tf_op jit(solution)/shard_map/spread/pallas_call | solution.py:172
  1.5 0.0 copy-start.10
  1.5 0.0 copy-start.11
  1.6 0.0 copy-start.9
  1.6 0.0 copy-start.4
  1.6 0.0 copy-start.6
  1.6 0.0 copy-start.7
  1.6 0.0 copy-start.8
  1.6 10.4 %all-to-all-start = ((bf16[8,32,768]{2,1,0:T(8,128)(2,1)}), bf16[8,32,768]{2,1,0:T(8,128)(2,1)S(1)}, u32[]{:S(2)}, u32[]{:S(2)}) async-start(bf16[8,32,768]{2,1,0:T(8,128)(2,1)} %spread.1), calls=%async_computation | async-start | bytes 786432 | tf_op jit(solution)/shard_map/all_to_all | solution.py:180
  12.0 0.0 copy-done.10
  12.0 0.0 copy-start.3
  12.0 0.2 copy.15.proj_ref
  12.1 0.0 copy-done.11
  12.2 0.1 copy.16.skip_ref
  12.2 7.8 %all-to-all-done = bf16[8,32,768]{2,1,0:T(8,128)(2,1)S(1)} async-done(((bf16[8,32,768]{2,1,0:T(8,128)(2,1)}), bf16[8,32,768]{2,1,0:T(8,128)(2,1)S(1)}, u32[]{:S(2)}, u32[]{:S(2)}) %all-to-all-start) | async-done | bytes 393248 | tf_op jit(solution)/shard_map/all_to_all | solution.py:180
  20.1 0.0 copy-done.9
  20.1 0.0 copy-start.1
  20.1 0.0 copy-start.2
  20.1 0.0 copy-start.5
  20.1 1.0 %project.1 = (bf16[64,8,128]{2,1,0:T(8,128)(2,1)}, f32[32,512]{1,0:T(8,128)S(1)}, f32[32,512]{1,0:T(8,128)S(1)}) custom-call(bf16[256,768]{1,0:T(8,128)(2,1)S(1)} %bitcast.5, bf16[3,256,32]{2,1,0:T(8,128)(2,1)S(1)} %copy.15.proj_ref, f32[32,512]{1,0:T(8,128)S(1)} %copy-done.9, f32[32,1]{1,0:T(8,128)S(1)} %copy.16.skip_ref), custom_call_target="tpu_custom_call" | custom-call | tf_op jit(solution)/shard_map/project/pallas_call | solution.py:182
  21.1 0.0 copy-start
  21.1 18.0 %all-to-all-start.1 = ((bf16[64,8,128]{2,1,0:T(8,128)(2,1)}), bf16[64,8,128]{2,1,0:T(8,128)(2,1)S(1)}, u32[]{:S(2)}, u32[]{:S(2)}) async-start(bf16[64,8,128]{2,1,0:T(8,128)(2,1)} %get-tuple-element.8), calls=%async_computation.1 | async-start | bytes 262144 | tf_op jit(solution)/shard_map/all_to_all | solution.py:196
  39.2 6.1 %all-to-all-done.1.recv_ref = bf16[64,8,128]{2,1,0:T(8,128)(2,1)S(1)} async-done(((bf16[64,8,128]{2,1,0:T(8,128)(2,1)}), bf16[64,8,128]{2,1,0:T(8,128)(2,1)S(1)}, u32[]{:S(2)}, u32[]{:S(2)}) %all-to-all-start.1) | async-done | bytes 131104 | tf_op jit(solution)/shard_map/all_to_all | solution.py:196
  45.2 0.0 copy-done.4
  45.2 0.0 copy-done.6
  45.2 0.0 copy-done.7
  45.2 0.0 copy-done.8
  45.3 0.0 copy-done.3
  45.3 0.0 copy-done.1
  45.3 0.0 copy-done.2
  45.3 0.0 copy-done.5
  45.3 0.0 copy-done
  45.3 1.6 %convolve.1 = bf16[32,4,128]{2,1,0:T(4,128)(2,1)S(1)} custom-call(s32[1]{0:T(128)} %bitcast.1.half_ref, bf16[64,8,128]{2,1,0:T(8,128)(2,1)S(1)} %all-to-all-done.1.recv_ref, bf16[512,256]{1,0:T(8,128)(2,1)S(1)} %copy-done, bf16[512,256]{1,0:T(8,128)(2,1)S(1)} %copy-done.1, bf16[256,512]{1,0:T(8,128)(2,1)S(1)} %copy-done.2, bf16[256,512]{1,0:T(8,128)(2,1)S(1)} %copy-done.3, ...), custom_call_target="tpu_custom_call" | custom-call | tf_op jit(solution)/shard_map/convolve/pallas_call | solution.py:199
  46.9 14.2 %all_to_all.20.recv_ref = bf16[32,4,128]{2,1,0:T(4,128)(2,1)S(1)} all-to-all(bf16[32,4,128]{2,1,0:T(4,128)(2,1)S(1)} %convolve.1), channel_id=1, replica_groups={{320,328,336,344,352,360,368,376,448,456,464,472,480,488,496,504,64,72,..., dimensions={0} | all-to-all | bytes 65536 | tf_op jit(solution)/shard_map/all_to_all | solution.py:212
  61.1 0.1 gate.1
  61.2 11.6 %all_to_all.21 = bf16[8,32,512]{2,1,0:T(8,128)(2,1)S(1)} all-to-all(bf16[8,32,512]{2,1,0:T(8,128)(2,1)S(1)} %gate.1), channel_id=1, replica_groups=mesh['context'=64,'tensor'=8] {'tensor'}, dimensions={0} | all-to-all | bytes 524288 | tf_op jit(solution)/shard_map/all_to_all | solution.py:224
  72.8 1.0 %convolution_convert_fusion = bf16[256,512]{1,0:T(8,128)(2,1)} fusion(bf16[256,512]{1,0:T(8,128)(2,1)S(1)} %bitcast.7, bf16[256,768]{1,0:T(8,128)(2,1)S(1)} %bitcast.6), kind=kOutput, calls=%fused_computation | convolution fusion | flops 67239936 | bytes 655360 | tf_op jit(solution)/shard_map/dot_general | solution.py:225
Async XLA Ops:
  1.5 10.4 %copy-start.10 = (bf16[3,256,32]{1,2,0:T(8,128)(2,1)S(1)}, bf16[3,256,32]{1,2,0:T(8,128)(2,1)}, u32[]{:S(2)}) copy-start(bf16[3,256,32]{1,2,0:T(8,128)(2,1)} %param.15) | copy-start | bytes 147460
  1.5 10.6 %copy-start.11 = (f32[32]{0:T(128)S(1)}, f32[32]{0:T(128)}, u32[]{:S(2)}) copy-start(f32[32]{0:T(128)} %param.17) | copy-start | bytes 388
  1.6 18.5 %copy-start.9 = (f32[32,512]{1,0:T(8,128)S(1)}, f32[32,512]{1,0:T(8,128)}, u32[]{:S(2)}) copy-start(f32[32,512]{1,0:T(8,128)} %filter_ref.1) | copy-start | bytes 196612
  1.6 43.7 %copy-start.4 = (f32[2,256,128]{2,1,0:T(8,128)S(1)}, f32[2,256,128]{2,1,0:T(8,128)}, u32[]{:S(2)}) copy-start(f32[2,256,128]{2,1,0:T(8,128)} %constant.61.clone.twist_ref) | copy-start | bytes 786436
  1.6 43.7 %copy-start.6 = (bf16[256,256]{1,0:T(8,128)(2,1)S(1)}, bf16[256,256]{1,0:T(8,128)(2,1)}, u32[]{:S(2)}) copy-start(bf16[256,256]{1,0:T(8,128)(2,1)} %constant.58.clone.in_lo) | copy-start | bytes 393220
  1.6 43.7 %copy-start.7 = (bf16[256,256]{1,0:T(8,128)(2,1)S(1)}, bf16[256,256]{1,0:T(8,128)(2,1)}, u32[]{:S(2)}) copy-start(bf16[256,256]{1,0:T(8,128)(2,1)} %constant.59.clone.out_hi) | copy-start | bytes 393220
  1.6 43.7 %copy-start.8 = (bf16[256,256]{1,0:T(8,128)(2,1)S(1)}, bf16[256,256]{1,0:T(8,128)(2,1)}, u32[]{:S(2)}) copy-start(bf16[256,256]{1,0:T(8,128)(2,1)} %constant.60.clone.out_lo) | copy-start | bytes 393220
  1.6 18.5 %all-to-all-start = ((bf16[8,32,768]{2,1,0:T(8,128)(2,1)}), bf16[8,32,768]{2,1,0:T(8,128)(2,1)S(1)}, u32[]{:S(2)}, u32[]{:S(2)}) async-start(bf16[8,32,768]{2,1,0:T(8,128)(2,1)} %spread.1), calls=%async_computation | async-start | bytes 786432 | tf_op jit(solution)/shard_map/all_to_all | solution.py:180
  12.0 33.3 %copy-start.3 = (bf16[256,512]{1,0:T(8,128)(2,1)S(1)}, bf16[256,512]{1,0:T(8,128)(2,1)}, u32[]{:S(2)}) copy-start(bf16[256,512]{1,0:T(8,128)(2,1)} %constant.56.clone.back_lo) | copy-start | bytes 786436
  20.1 25.2 %copy-start.1 = (bf16[512,256]{1,0:T(8,128)(2,1)S(1)}, bf16[512,256]{1,0:T(8,128)(2,1)}, u32[]{:S(2)}) copy-start(bf16[512,256]{1,0:T(8,128)(2,1)} %constant.54.clone.fwd_lo) | copy-start | bytes 786436
  20.1 25.2 %copy-start.2 = (bf16[256,512]{1,0:T(8,128)(2,1)S(1)}, bf16[256,512]{1,0:T(8,128)(2,1)}, u32[]{:S(2)}) copy-start(bf16[256,512]{1,0:T(8,128)(2,1)} %constant.55.clone.back_hi) | copy-start | bytes 786436
  20.1 25.2 %copy-start.5 = (bf16[256,256]{1,0:T(8,128)(2,1)S(1)}, bf16[256,256]{1,0:T(8,128)(2,1)}, u32[]{:S(2)}) copy-start(bf16[256,256]{1,0:T(8,128)(2,1)} %constant.57.clone.in_hi) | copy-start | bytes 393220
  21.1 24.2 %copy-start = (bf16[512,256]{1,0:T(8,128)(2,1)S(1)}, bf16[512,256]{1,0:T(8,128)(2,1)}, u32[]{:S(2)}) copy-start(bf16[512,256]{1,0:T(8,128)(2,1)} %constant.53.clone.fwd_hi) | copy-start | bytes 786436
  21.1 24.1 %all-to-all-start.1 = ((bf16[64,8,128]{2,1,0:T(8,128)(2,1)}), bf16[64,8,128]{2,1,0:T(8,128)(2,1)S(1)}, u32[]{:S(2)}, u32[]{:S(2)}) async-start(bf16[64,8,128]{2,1,0:T(8,128)(2,1)} %get-tuple-element.8), calls=%async_computation.1 | async-start | bytes 262144 | tf_op jit(solution)/shard_map/all_to_all | solution.py:196

commit v3 on v2

--- a/solution.py
+++ b/solution.py
@@ -19,9 +19,11 @@
 TURN = 2
 HALVES = [
     [(outer + TURN) % LINES * RING + inner for outer in range(LINES) for inner in ring]
-    for ring in (range(RING // 2, RING), range(RING // 2 - 1, -1, -1))
+    for ring in ((10, 11, 12, 13, 14, 15, 8, 9), (7, 6, 5, 4, 3, 2, 1, 0))
 ]
 ORDER = HALVES[0] + HALVES[1]
+
+GROUP = [4, 5, 6, 7, 0, 1, 2, 3]
 
 
 def split_table(table):
@@ -77,16 +79,20 @@
     gathered_ref, proj_ref, filter_ref, skip_ref, send_ref, gate_ref, direct_ref, rows_ref
 ):
     channels, tok_len = filter_ref.shape
-    sequence = gathered_ref[:, :tok_len]
-    first, gate, value = [
-        lax.dot_general(
-            proj_ref[index], sequence, (((0,), (0,)), ((), ())), preferred_element_type=jnp.float32
-        )
-        for index in range(3)
-    ]
+    sequence = jnp.concatenate(
+        [
+            gathered_ref[place * channels : (place + 1) * channels, :tok_len]
+            for place in np.argsort(GROUP).tolist()
+        ],
+        axis=0,
+    )
+    first, gate, value = [dot(proj_ref[index], sequence) for index in range(3)]
     gated = value * first
     gate_ref[...] = gate
-    direct_ref[...] = skip_ref[...] * gated
+    place = lax.broadcasted_iota(jnp.int32, (channels, channels), 0)
+    other = lax.broadcasted_iota(jnp.int32, (channels, channels), 1)
+    skip = jnp.sum(jnp.where(place == other, skip_ref[...], 0.0), axis=1, keepdims=True)
+    direct_ref[...] = skip * gated
     for piece in range(PIECE):
         cut = slice(piece * LANES, (piece + 1) * LANES)
         for half in range(2):
@@ -97,7 +103,7 @@
 
 
 def convolve_kernel(
-    half_ref, recv_ref, fwd_hi, fwd_lo, back_hi, back_lo, in_hi, in_lo, out_hi, out_lo, twist_ref,
+    recv_ref, fwd_hi, fwd_lo, back_hi, back_lo, in_hi, in_lo, out_hi, out_lo, twist_ref,
     send_ref, rows_ref, result_ref,
 ):
     rows_ref[...] = recv_ref[...].astype(jnp.float32)
@@ -142,9 +148,10 @@
             [real * cos_part - imag * sin_part, imag * cos_part + real * sin_part], axis=0
         )
     )
-    span = pl.ds(pl.multiple_of(half_ref[0] * (ROWS // 2), ROWS // 2), ROWS // 2)
-    left_hi, left_lo = back_hi[span, :], back_lo[span, :]
-    result = dot(left_hi, upper) + dot(left_hi, lower) + dot(left_lo, upper)
+    half = 1 - lax.axis_index("context") % RING // (RING // 2)
+    span = pl.ds(pl.multiple_of(half * (ROWS // 2), ROWS // 2), ROWS // 2)
+    both = dot(back_hi[span, :], jnp.concatenate([upper, lower], axis=1))
+    result = both[:, :LANES] + both[:, LANES:] + dot(back_lo[span, :], upper)
     for piece in range(PIECE):
         result_ref[:, piece, :] = result[piece * CHANNELS : (piece + 1) * CHANNELS]
     send_ref[...] = result_ref[...].astype(jnp.bfloat16)
@@ -167,7 +174,6 @@
     width = proj_out.shape[1]
     groups = lax.axis_size("tensor")
     ranks = lax.axis_size("context")
-    half = (1 - lax.axis_index("context") % RING // (RING // 2)).astype(jnp.int32).reshape(1)
 
     send = pl.pallas_call(
         spread_kernel,
@@ -177,7 +183,8 @@
         name="spread",
     )(sequence, proj_out)
 
-    gathered = lax.all_to_all(send, "tensor", 0, 0, tiled=True).reshape(width, tok_len + width)
+    gathered = lax.all_to_all(send, "tensor", 0, 0, axis_index_groups=[GROUP], tiled=True)
+    gathered = gathered.reshape(width, tok_len + width)
 
     send, gate, direct = pl.pallas_call(
         project_kernel,
@@ -191,7 +198,7 @@
         scratch_shapes=[pltpu.VMEM((ranks, 2 * PIECE, LANES), jnp.float32)],
         compiler_params=pltpu.CompilerParams(vmem_limit_bytes=16 * 2**20),
         name="project",
-    )(gathered, proj_in, conv_filter, skip_gain.reshape(channels, 1))
+    )(gathered, jnp.swapaxes(proj_in, 1, 2), conv_filter, skip_gain.reshape(1, channels))
 
     recv = lax.all_to_all(send, "context", 0, 0, axis_index_groups=[ORDER], tiled=True)
 
@@ -199,7 +206,7 @@
     send = pl.pallas_call(
         convolve_kernel,
         out_shape=pltpu.VMEM((channels, PIECE, LANES), jnp.bfloat16),
-        in_specs=[pl.BlockSpec(memory_space=pltpu.SMEM)] + whole(1 + len(constants)),
+        in_specs=whole(1 + len(constants)),
         out_specs=whole(1)[0],
         scratch_shapes=[
             pltpu.VMEM((ranks, 2 * PIECE, LANES), jnp.float32),
@@ -207,7 +214,7 @@
         ],
         compiler_params=pltpu.CompilerParams(vmem_limit_bytes=24 * 2**20),
         name="convolve",
-    )(half, recv, *constants)
+    )(recv, *constants)
 
     recv = lax.all_to_all(send, "context", 0, 0, axis_index_groups=HALVES, tiled=True)
 
@@ -221,10 +228,10 @@
         name="gate",
     )(recv, gate, direct)
 
-    out_gated = lax.all_to_all(send, "tensor", 0, 0, tiled=True).reshape(width, tok_len)
+    out_gated = lax.all_to_all(send, "tensor", 0, 0, axis_index_groups=[GROUP], tiled=True)
     mixed = lax.dot_general(
         gathered[:, tok_len:],
-        out_gated,
+        out_gated.reshape(width, tok_len),
         (((0,), (0,)), ((), ())),
         preferred_element_type=jnp.float32,
     )

time: 74.1 us -> 70.1 us (0.946)
  blocking collectives: 25.8 us -> 65.8 us
  starting transfers between devices: 28.4 us -> 0 us
  waiting for transfers between devices: 13.9 us -> 0 us
  Pallas kernels: 4.2 us -> 2.8 us
    all_to_all x1 -> x3, blocking collectives: 11.6 us -> 51.4 us  [the longest x2 28.3 us: shards(): lax.all_to_all(send, 'tensor', 0, 0, axis_index_groups=[GROUP], tiled=True)]
    all_to_all x2 -> x0, starting transfers between devices: 28.4 us -> none  [the longest x1 18 us: shards(): lax.all_to_all(send, 'context', 0, 0, axis_index_groups=[ORDER], tiled=True)]
    all_to_all x2 -> x0, waiting for transfers between devices: 13.9 us -> none  [the longest x1 7.83 us: shards(): lax.all_to_all(send, 'tensor', 0, 0, tiled=True)]
  transfers between devices with their start and end apart: 2 -> 0, of which waited for: 2 -> 0; matrix products, arithmetic and copies ran while one was open for 0% -> 0% of each run, Pallas kernels for 0% -> 0%
where the time goes in v3:
time: 70.1 us; the launch traced here: 69.8 us
  blocking collectives  65.8 us (94%)
  Pallas kernels  2.8 us (4%)
  matrix products  0.95 us (1%)
    all_to_all x2, blocking collectives, shards(): lax.all_to_all(send, 'tensor', 0, 0, axis_index_groups=[GROUP], tiled=True)  28.3 us
    all_to_all x1, blocking collectives, shards(): lax.all_to_all(send, 'context', 0, 0, axis_index_groups=[ORDER], tiled=True)  23.1 us
    all_to_all x1, blocking collectives, shards(): lax.all_to_all(send, 'context', 0, 0, axis_index_groups=HALVES, tiled=True)  14.4 us
    pallas_call x1, Pallas kernels, shards(): pl.pallas_call(convolve_kernel, out_shape=pltpu.VMEM((channels, PIECE, LA...  1.53 us

profile of v3, /device:TPU:1, one launch (start us, length us, event | category | flops | bytes accessed | tf_op | source)
XLA Modules:
  0.0 69.8 jit_solution(3015023090769483591)
XLA Ops:
  0.0 0.0 copy-start.9
  0.0 0.0 copy-start.10
  0.0 0.0 copy-start.11
  0.0 0.0 copy-start.6
  0.0 0.0 copy-start.7
  0.0 0.0 copy-start.8
  0.0 0.9 %spread.1 = bf16[8,32,768]{2,1,0:T(8,128)(2,1)S(1)} custom-call(bf16[32,512]{1,0:T(8,128)(2,1)} %sequence_ref.1, bf16[32,256]{1,0:T(8,128)(2,1)} %proj_ref.1), custom_call_target="tpu_custom_call" | custom-call | tf_op jit(solution)/shard_map/spread/pallas_call | solution.py:178
  0.9 0.0 copy-start.2
  0.9 0.0 copy-start.3
  0.9 0.0 copy-start.4
  1.0 16.5 %all_to_all.20 = bf16[8,32,768]{2,1,0:T(8,128)(2,1)S(1)} all-to-all(bf16[8,32,768]{2,1,0:T(8,128)(2,1)S(1)} %spread.1), channel_id=1, replica_groups={{4,5,6,7,0,1,2,3},{12,13,14,15,8,9,10,11},{20,21,22,23,16,17,18,19},{28..., dimensions={0} | all-to-all | bytes 786432 | tf_op jit(solution)/shard_map/all_to_all | solution.py:186
  17.5 0.0 copy-done.9
  17.5 0.0 copy-done.10
  17.5 0.0 copy-done.11
  17.5 0.0 copy-start
  17.5 0.0 copy-start.1
  17.5 0.3 project.1
  17.9 0.0 copy-start.5
  17.9 23.1 %all_to_all.21.recv_ref = bf16[64,8,128]{2,1,0:T(8,128)(2,1)S(1)} all-to-all(bf16[64,8,128]{2,1,0:T(8,128)(2,1)S(1)} %get-tuple-element.8), channel_id=1, replica_groups={{336,344,352,360,368,376,320,328,464,472,480,488,496,504,448,456,80,88,..., dimensions={0} | all-to-all | bytes 262144 | tf_op jit(solution)/shard_map/all_to_all | solution.py:203
  40.9 0.0 copy-done.6
  40.9 0.0 copy-done.7
  40.9 0.0 copy-done.8
  40.9 0.0 copy-done.2
  40.9 0.0 copy-done.3
  41.0 0.0 copy-done.4
  41.0 0.0 copy-done
  41.0 0.0 copy-done.1
  41.0 0.0 copy-done.5
  41.0 1.5 %convolve.1 = bf16[32,4,128]{2,1,0:T(4,128)(2,1)S(1)} custom-call(bf16[64,8,128]{2,1,0:T(8,128)(2,1)S(1)} %all_to_all.21.recv_ref, bf16[512,256]{1,0:T(8,128)(2,1)S(1)} %copy-done.4, bf16[512,256]{1,0:T(8,128)(2,1)S(1)} %copy-done.3, bf16[256,512]{1,0:T(8,128)(2,1)S(1)} %copy-done.2, bf16[256,512]{1,0:T(8,128)(2,1)S(1)} %copy-done.1, ...), custom_call_target="tpu_custom_call" | custom-call | tf_op jit(solution)/shard_map/convolve/pallas_call | solution.py:206
  42.5 14.4 %all_to_all.22.recv_ref = bf16[32,4,128]{2,1,0:T(4,128)(2,1)S(1)} all-to-all(bf16[32,4,128]{2,1,0:T(4,128)(2,1)S(1)} %convolve.1), channel_id=1, replica_groups={{336,344,352,360,368,376,320,328,464,472,480,488,496,504,448,456,80,88,..., dimensions={0} | all-to-all | bytes 65536 | tf_op jit(solution)/shard_map/all_to_all | solution.py:219
  57.0 0.1 gate.1
  57.0 11.8 %all_to_all.23 = bf16[8,32,512]{2,1,0:T(8,128)(2,1)S(1)} all-to-all(bf16[8,32,512]{2,1,0:T(8,128)(2,1)S(1)} %gate.1), channel_id=1, replica_groups={{4,5,6,7,0,1,2,3},{12,13,14,15,8,9,10,11},{20,21,22,23,16,17,18,19},{28..., dimensions={0} | all-to-all | bytes 524288 | tf_op jit(solution)/shard_map/all_to_all | solution.py:231
  68.8 1.0 %convolution_convert_fusion = bf16[256,512]{1,0:T(8,128)(2,1)} fusion(bf16[256,512]{1,0:T(8,128)(2,1)S(1)} %bitcast.9, bf16[256,768]{1,0:T(8,128)(2,1)S(1)} %bitcast.6), kind=kOutput, calls=%fused_computation | convolution fusion | flops 67239936 | bytes 655360 | tf_op jit(solution)/shard_map/dot_general | solution.py:232
Async XLA Ops:
  0.0 17.5 %copy-start.9 = (f32[32,512]{1,0:T(8,128)S(1)}, f32[32,512]{1,0:T(8,128)}, u32[]{:S(2)}) copy-start(f32[32,512]{1,0:T(8,128)} %filter_ref.1) | copy-start | bytes 196612
  0.0 17.5 %copy-start.10 = (bf16[3,256,32]{1,2,0:T(8,128)(2,1)S(1)}, bf16[3,256,32]{1,2,0:T(8,128)(2,1)}, u32[]{:S(2)}) copy-start(bf16[3,256,32]{1,2,0:T(8,128)(2,1)} %param.15) | copy-start | bytes 147460
  0.0 17.5 %copy-start.11 = (f32[32]{0:T(128)S(1)}, f32[32]{0:T(128)}, u32[]{:S(2)}) copy-start(f32[32]{0:T(128)} %param.17) | copy-start | bytes 388
  0.0 40.9 %copy-start.6 = (bf16[256,256]{1,0:T(8,128)(2,1)S(1)}, bf16[256,256]{1,0:T(8,128)(2,1)}, u32[]{:S(2)}) copy-start(bf16[256,256]{1,0:T(8,128)(2,1)} %constant.24.clone.out_hi) | copy-start | bytes 393220
  0.0 40.9 %copy-start.7 = (bf16[256,256]{1,0:T(8,128)(2,1)S(1)}, bf16[256,256]{1,0:T(8,128)(2,1)}, u32[]{:S(2)}) copy-start(bf16[256,256]{1,0:T(8,128)(2,1)} %constant.23.clone.in_lo) | copy-start | bytes 393220
  0.0 40.9 %copy-start.8 = (bf16[256,256]{1,0:T(8,128)(2,1)S(1)}, bf16[256,256]{1,0:T(8,128)(2,1)}, u32[]{:S(2)}) copy-start(bf16[256,256]{1,0:T(8,128)(2,1)} %constant.22.clone.in_hi) | copy-start | bytes 393220
  0.9 40.0 %copy-start.2 = (bf16[256,512]{1,0:T(8,128)(2,1)S(1)}, bf16[256,512]{1,0:T(8,128)(2,1)}, u32[]{:S(2)}) copy-start(bf16[256,512]{1,0:T(8,128)(2,1)} %constant.20.clone.back_hi) | copy-start | bytes 786436
  0.9 40.0 %copy-start.3 = (bf16[512,256]{1,0:T(8,128)(2,1)S(1)}, bf16[512,256]{1,0:T(8,128)(2,1)}, u32[]{:S(2)}) copy-start(bf16[512,256]{1,0:T(8,128)(2,1)} %constant.19.clone.fwd_lo) | copy-start | bytes 786436
  0.9 40.0 %copy-start.4 = (bf16[512,256]{1,0:T(8,128)(2,1)S(1)}, bf16[512,256]{1,0:T(8,128)(2,1)}, u32[]{:S(2)}) copy-start(bf16[512,256]{1,0:T(8,128)(2,1)} %constant.18.clone.fwd_hi) | copy-start | bytes 786436
  17.5 23.5 %copy-start = (f32[2,256,128]{2,1,0:T(8,128)S(1)}, f32[2,256,128]{2,1,0:T(8,128)}, u32[]{:S(2)}) copy-start(f32[2,256,128]{2,1,0:T(8,128)} %constant.26.clone.twist_ref) | copy-start | bytes 786436
  17.5 23.5 %copy-start.1 = (bf16[256,512]{1,0:T(8,128)(2,1)S(1)}, bf16[256,512]{1,0:T(8,128)(2,1)}, u32[]{:S(2)}) copy-start(bf16[256,512]{1,0:T(8,128)(2,1)} %constant.21.clone.back_lo) | copy-start | bytes 786436
  17.9 23.1 %copy-start.5 = (bf16[256,256]{1,0:T(8,128)(2,1)S(1)}, bf16[256,256]{1,0:T(8,128)(2,1)}, u32[]{:S(2)}) copy-start(bf16[256,256]{1,0:T(8,128)(2,1)} %constant.25.clone.out_lo) | copy-start | bytes 393220

commit v4 on v3

--- a/solution.py
+++ b/solution.py
@@ -19,7 +19,7 @@
 TURN = 2
 HALVES = [
     [(outer + TURN) % LINES * RING + inner for outer in range(LINES) for inner in ring]
-    for ring in ((10, 11, 12, 13, 14, 15, 8, 9), (7, 6, 5, 4, 3, 2, 1, 0))
+    for ring in ((10, 11, 12, 13, 14, 15, 8, 9), (6, 7, 5, 4, 3, 2, 1, 0))
 ]
 ORDER = HALVES[0] + HALVES[1]
 
@@ -68,15 +68,39 @@
     return upper, lower
 
 
-def spread_kernel(sequence_ref, proj_ref, send_ref):
+def halves(part, rows):
+    middle = rows // 2
+    return jnp.concatenate([part(slice(0, middle)), part(slice(middle, rows))], axis=0)
+
+
+def inner_transform(value, table_hi, table_lo):
+    upper, lower = split_value(value)
+    return halves(
+        lambda cut: dot(upper[cut], table_hi[...])
+        + dot(lower[cut], table_hi[...])
+        + dot(upper[cut], table_lo[...]),
+        value.shape[0],
+    )
+
+
+def spread_kernel(
+    sequence_ref, proj_ref, filter_ref, skip_ref, out_ref,
+    send_ref, proj_copy, filter_copy, skip_copy, out_copy,
+):
     tok_len = sequence_ref.shape[1]
     for copy in range(send_ref.shape[0]):
         send_ref[copy, :, :tok_len] = sequence_ref[...]
-        send_ref[copy, :, tok_len:] = proj_ref[...]
+        if send_ref.shape[2] > tok_len:
+            send_ref[copy, :, tok_len:] = out_ref[...]
+    proj_copy[...] = proj_ref[...]
+    filter_copy[...] = filter_ref[...]
+    skip_copy[...] = skip_ref[...]
+    out_copy[...] = out_ref[...]
 
 
 def project_kernel(
-    gathered_ref, proj_ref, filter_ref, skip_ref, send_ref, gate_ref, direct_ref, rows_ref
+    gathered_ref, proj_ref, filter_ref, skip_ref, own_ref,
+    send_ref, gate_ref, direct_ref, out_ref, rows_ref,
 ):
     channels, tok_len = filter_ref.shape
     sequence = jnp.concatenate(
@@ -93,6 +117,11 @@
     other = lax.broadcasted_iota(jnp.int32, (channels, channels), 1)
     skip = jnp.sum(jnp.where(place == other, skip_ref[...], 0.0), axis=1, keepdims=True)
     direct_ref[...] = skip * gated
+    if gathered_ref.shape[1] > tok_len:
+        out_ref[...] = gathered_ref[:, tok_len:]
+    else:
+        out_ref[:channels] = own_ref[...]
+        out_ref[channels:] = jnp.zeros_like(out_ref[channels:])
     for piece in range(PIECE):
         cut = slice(piece * LANES, (piece + 1) * LANES)
         for half in range(2):
@@ -116,7 +145,7 @@
     ).astype(jnp.bfloat16)
     cos_part = twist_ref[0]
     sin_part = twist_ref[1]
-    outer = dot(fwd_hi[...], both) + dot(fwd_lo[...], both)
+    outer = halves(lambda cut: dot(fwd_hi[cut], both) + dot(fwd_lo[cut], both), 2 * ROWS)
     real, imag = outer[:ROWS], outer[ROWS:]
     turned = []
     for cut in (slice(0, LANES), slice(LANES, 2 * LANES)):
@@ -129,8 +158,7 @@
                 axis=1,
             )
         )
-    upper, lower = split_value(jnp.concatenate(turned, axis=0))
-    spectra = dot(upper, in_hi[...]) + dot(lower, in_hi[...]) + dot(upper, in_lo[...])
+    spectra = inner_transform(jnp.concatenate(turned, axis=0), in_hi, in_lo)
     source_real, source_imag = spectra[:ROWS, :LANES], spectra[:ROWS, LANES:]
     filter_real, filter_imag = spectra[ROWS:, :LANES], spectra[ROWS:, LANES:]
     product = jnp.concatenate(
@@ -140,8 +168,7 @@
         ],
         axis=1,
     )
-    upper, lower = split_value(product)
-    inner = dot(upper, out_hi[...]) + dot(lower, out_hi[...]) + dot(upper, out_lo[...])
+    inner = inner_transform(product, out_hi, out_lo)
     real, imag = inner[:, :LANES], inner[:, LANES:]
     upper, lower = split_value(
         jnp.concatenate(
@@ -157,12 +184,34 @@
     send_ref[...] = result_ref[...].astype(jnp.bfloat16)
 
 
-def gate_kernel(recv_ref, gate_ref, direct_ref, send_ref, rows_ref):
+def gate_kernel(recv_ref, gate_ref, direct_ref, out_ref, send_ref, rows_ref):
+    channels, tok_len = gate_ref.shape
     rows_ref[...] = recv_ref[...].astype(jnp.float32)
     convolved = jnp.concatenate([rows_ref[:, piece, :] for piece in range(PIECE)], axis=1)
     out_gated = ((convolved + direct_ref[...]) * gate_ref[...]).astype(jnp.bfloat16)
     for copy in range(send_ref.shape[0]):
-        send_ref[copy] = out_gated
+        send_ref[copy, :, :tok_len] = out_gated
+        if send_ref.shape[2] > tok_len:
+            send_ref[copy, :, tok_len:] = out_ref[:channels]
+
+
+def mix_kernel(out_ref, gathered_ref, mixed_ref):
+    tok_len = mixed_ref.shape[1]
+    late = gathered_ref.shape[1] > tok_len
+    mixed_ref[...] = lax.dot_general(
+        gathered_ref[:, tok_len:] if late else out_ref[...],
+        gathered_ref[:, :tok_len],
+        (((0,), (0,)), ((), ())),
+        preferred_element_type=jnp.float32,
+    ).astype(jnp.bfloat16)
+
+
+def near(*arrays):
+    return [pltpu.with_memory_space_constraint(array, pltpu.VMEM) for array in arrays]
+
+
+def far(*arrays):
+    return [pltpu.with_memory_space_constraint(array, pltpu.HBM) for array in arrays]
 
 
 def whole(count):
@@ -175,30 +224,47 @@
     groups = lax.axis_size("tensor")
     ranks = lax.axis_size("context")
 
-    send = pl.pallas_call(
-        spread_kernel,
-        out_shape=pltpu.VMEM((groups, channels, tok_len + width), jnp.bfloat16),
-        in_specs=whole(2),
-        out_specs=whole(1)[0],
-        name="spread",
-    )(sequence, proj_out)
-
-    gathered = lax.all_to_all(send, "tensor", 0, 0, axis_index_groups=[GROUP], tiled=True)
-    gathered = gathered.reshape(width, tok_len + width)
-
-    send, gate, direct = pl.pallas_call(
-        project_kernel,
-        out_shape=(
-            pltpu.VMEM((ranks, 2 * PIECE, LANES), jnp.bfloat16),
-            pltpu.VMEM((channels, tok_len), jnp.float32),
-            pltpu.VMEM((channels, tok_len), jnp.float32),
-        ),
-        in_specs=whole(4),
-        out_specs=tuple(whole(3)),
-        scratch_shapes=[pltpu.VMEM((ranks, 2 * PIECE, LANES), jnp.float32)],
-        compiler_params=pltpu.CompilerParams(vmem_limit_bytes=16 * 2**20),
-        name="project",
-    )(gathered, jnp.swapaxes(proj_in, 1, 2), conv_filter, skip_gain.reshape(1, channels))
+    early = lax.axis_index("context") % RING < RING // 2
+
+    def begin(lanes):
+        operands = [
+            sequence,
+            jnp.swapaxes(proj_in, 1, 2),
+            conv_filter,
+            skip_gain.reshape(1, channels),
+            proj_out,
+        ]
+        send, *local = pl.pallas_call(
+            spread_kernel,
+            out_shape=(
+                pltpu.VMEM((groups, channels, lanes), jnp.bfloat16),
+                *[pltpu.VMEM(operand.shape, operand.dtype) for operand in operands[1:]],
+            ),
+            in_specs=whole(5),
+            out_specs=tuple(whole(5)),
+            name="spread",
+        )(*far(*operands))
+        gathered = lax.all_to_all(send, "tensor", 0, 0, axis_index_groups=[GROUP], tiled=True)
+        return tuple(
+            pl.pallas_call(
+                project_kernel,
+                out_shape=(
+                    pltpu.VMEM((ranks, 2 * PIECE, LANES), jnp.bfloat16),
+                    pltpu.VMEM((channels, tok_len), jnp.float32),
+                    pltpu.VMEM((channels, tok_len), jnp.float32),
+                    pltpu.VMEM((width, width), jnp.bfloat16),
+                ),
+                in_specs=whole(5),
+                out_specs=tuple(whole(4)),
+                scratch_shapes=[pltpu.VMEM((ranks, 2 * PIECE, LANES), jnp.float32)],
+                compiler_params=pltpu.CompilerParams(vmem_limit_bytes=16 * 2**20),
+                name="project",
+            )(*near(gathered.reshape(width, lanes), *local))
+        )
+
+    send, gate, direct, proj_full = lax.cond(
+        early, lambda: begin(tok_len + width), lambda: begin(tok_len)
+    )
 
     recv = lax.all_to_all(send, "context", 0, 0, axis_index_groups=[ORDER], tiled=True)
 
@@ -218,24 +284,27 @@
 
     recv = lax.all_to_all(send, "context", 0, 0, axis_index_groups=HALVES, tiled=True)
 
-    send = pl.pallas_call(
-        gate_kernel,
-        out_shape=pltpu.VMEM((groups, channels, tok_len), jnp.bfloat16),
-        in_specs=whole(3),
-        out_specs=whole(1)[0],
-        scratch_shapes=[pltpu.VMEM((channels, PIECE, LANES), jnp.float32)],
-        compiler_params=pltpu.CompilerParams(vmem_limit_bytes=16 * 2**20),
-        name="gate",
-    )(recv, gate, direct)
-
-    out_gated = lax.all_to_all(send, "tensor", 0, 0, axis_index_groups=[GROUP], tiled=True)
-    mixed = lax.dot_general(
-        gathered[:, tok_len:],
-        out_gated.reshape(width, tok_len),
-        (((0,), (0,)), ((), ())),
-        preferred_element_type=jnp.float32,
-    )
-    return mixed.astype(jnp.bfloat16)
+    def finish(lanes):
+        send = pl.pallas_call(
+            gate_kernel,
+            out_shape=pltpu.VMEM((groups, channels, lanes), jnp.bfloat16),
+            in_specs=whole(4),
+            out_specs=whole(1)[0],
+            scratch_shapes=[pltpu.VMEM((channels, PIECE, LANES), jnp.float32)],
+            compiler_params=pltpu.CompilerParams(vmem_limit_bytes=16 * 2**20),
+            name="gate",
+        )(*near(recv, gate, direct, proj_full))
+        gathered = lax.all_to_all(send, "tensor", 0, 0, axis_index_groups=[GROUP], tiled=True)
+        return pl.pallas_call(
+            mix_kernel,
+            out_shape=pltpu.HBM((width, tok_len), jnp.bfloat16),
+            in_specs=whole(2),
+            out_specs=whole(1)[0],
+            compiler_params=pltpu.CompilerParams(vmem_limit_bytes=16 * 2**20),
+            name="mix",
+        )(*near(proj_full, gathered.reshape(width, lanes)))
+
+    return lax.cond(early, lambda: finish(tok_len), lambda: finish(tok_len + width))
 
 
 def solution(mesh):

time: 70.1 us -> 67.6 us (0.964)
  blocking collectives: 65.8 us -> 63.6 us
  matrix products: 0.95 us -> 0 us
  Pallas kernels: 2.8 us -> 3.54 us
    pallas_call x3 -> x4, Pallas kernels: 1.27 us -> 2.37 us  [the longest x1 1.02 us: begin(): pl.pallas_call(spread_kernel, out_shape=(pltpu.VMEM((groups, channels, la...]
    all_to_all x1, blocking collectives: 14.4 us -> 13.4 us  [shards(): lax.all_to_all(send, 'context', 0, 0, axis_index_groups=HALVES, tiled=True)]
    dot_general x1 -> x0, matrix products: 0.95 us -> none  [shards(): lax.dot_general(gathered[:, tok_len:], out_gated.reshape(width, tok_len),...]
    all_to_all x2, blocking collectives: 28.3 us -> 27.5 us  [the longest x1 16.4 us: begin(): lax.all_to_all(send, 'tensor', 0, 0, axis_index_groups=[GROUP], tiled=True)]
where the time goes in v4:
time: 67.6 us; the launch traced here: 67.3 us
  blocking collectives  63.6 us (94%)
  Pallas kernels  3.54 us (5%)
    all_to_all x1, blocking collectives, shards(): lax.all_to_all(send, 'context', 0, 0, axis_index_groups=[ORDER], tiled=True)  22.7 us
    all_to_all x1, blocking collectives, begin(): lax.all_to_all(send, 'tensor', 0, 0, axis_index_groups=[GROUP], tiled=True)  16.4 us
    all_to_all x1, blocking collectives, shards(): lax.all_to_all(send, 'context', 0, 0, axis_index_groups=HALVES, tiled=True)  13.4 us
    all_to_all x1, blocking collectives, finish(): lax.all_to_all(send, 'tensor', 0, 0, axis_index_groups=[GROUP], tiled=True)  11.1 us

profile of v4, /device:TPU:1, one launch (start us, length us, event | category | flops | bytes accessed | tf_op | source)
XLA Modules:
  0.0 67.3 jit_solution(5175878712492837985)
XLA Ops:
  0.0 0.0 copy-start.1
  0.0 0.0 copy-start.2
  0.0 0.0 copy-start.3
  0.0 0.0 copy-start.4
  0.0 0.0 copy-start.5
  0.0 0.0 copy-start.6
  0.0 0.0 copy-start.7
  0.1 0.0 copy-start.8
  0.1 17.8 %conditional.2 = ((bf16[64,8,128]{2,1,0:T(8,128)(2,1)S(1)}, f32[32,512]{1,0:T(8,128)S(1)}, f32[32,512]{1,0:T(8,128)S(1)}, bf16[256,256]{1,0:T(8,128)(2,1)S(1)})) conditional(s32[]{:T(128)} %convert_element_type.4, (bf16[3,256,32]{1,2,0:T(8,128)(2,1)}, f32[32]{0:T(128)}, bf16[32,512]{1,0:T(8,128)(2,1)}, f32[32,512]{1,0:T(8,128)}, ...), branch_computations={%region_0.1_spmd, %region_1.2_spmd} | conditional | bytes 786440 | solution.py:265
  0.1 1.0 %spread.3 = (bf16[8,32,768]{2,1,0:T(8,128)(2,1)S(1)}, bf16[3,32,256]{2,1,0:T(8,128)(2,1)S(1)}, f32[32,512]{1,0:T(8,128)S(1)}, f32[1,32]{1,0:T(1,128)S(1)}, bf16[32,256]{1,0:T(8,128)(2,1)S(1)}) custom-call(bf16[32,512]{1,0:T(8,128)(2,1)} %get-tuple-element.54.sequence_ref, bf16[3,32,256]{2,1,0:T(8,128)(2,1)} %bitcast.13, ...), custom_call_target="tpu_custom_call" | custom-call | tf_op jit(solution)/shard_map/cond/branch_1_fun/spread/pallas_call | solution.py:237
  1.1 16.4 %all_to_all.27 = bf16[8,32,768]{2,1,0:T(8,128)(2,1)S(1)} all-to-all(bf16[8,32,768]{2,1,0:T(8,128)(2,1)S(1)} %get-tuple-element.59), channel_id=1, replica_groups={{4,5,6,7,0,1,2,3},{12,13,14,15,8,9,10,11},{20,21,22,23,16,17,18,19},{28..., dimensions={0} | all-to-all | bytes 786432 | tf_op jit(solution)/shard_map/cond/branch_1_fun/all_to_all | solution.py:247
  17.5 0.3 project.3
  17.9 0.0 copy-start
  17.9 22.7 %all_to_all.30.recv_ref = bf16[64,8,128]{2,1,0:T(8,128)(2,1)S(1)} all-to-all(bf16[64,8,128]{2,1,0:T(8,128)(2,1)S(1)} %get-tuple-element.76), channel_id=1, replica_groups={{336,344,352,360,368,376,320,328,464,472,480,488,496,504,448,456,80,88,..., dimensions={0} | all-to-all | bytes 262144 | tf_op jit(solution)/shard_map/all_to_all | solution.py:269
  40.6 0.0 copy-done.1
  40.6 0.0 copy-done.2
  40.6 0.0 copy-done.3
  40.6 0.0 copy-done.4
  40.6 0.0 copy-done.5
  40.7 0.0 copy-done.6
  40.7 0.0 copy-done.7
  40.7 0.0 copy-done.8
  40.7 0.0 copy-done
  40.7 1.2 %convolve.1 = bf16[32,4,128]{2,1,0:T(4,128)(2,1)S(1)} custom-call(bf16[64,8,128]{2,1,0:T(8,128)(2,1)S(1)} %all_to_all.30.recv_ref, bf16[512,256]{1,0:T(8,128)(2,1)S(1)} %copy-done.4, bf16[512,256]{1,0:T(8,128)(2,1)S(1)} %copy-done.3, bf16[256,512]{1,0:T(8,128)(2,1)S(1)} %copy-done.2, bf16[256,512]{1,0:T(8,128)(2,1)S(1)} %copy-done.1, ...), custom_call_target="tpu_custom_call" | custom-call | tf_op jit(solution)/shard_map/convolve/pallas_call | solution.py:272
  41.9 13.4 %all_to_all.31 = bf16[32,4,128]{2,1,0:T(4,128)(2,1)S(1)} all-to-all(bf16[32,4,128]{2,1,0:T(4,128)(2,1)S(1)} %convolve.1), channel_id=1, replica_groups={{336,344,352,360,368,376,320,328,464,472,480,488,496,504,448,456,80,88,..., dimensions={0} | all-to-all | bytes 65536 | tf_op jit(solution)/shard_map/all_to_all | solution.py:285
  55.2 12.1 %conditional.3 = (bf16[256,512]{1,0:T(8,128)(2,1)}) conditional(s32[]{:T(128)} %convert_element_type.4, (bf16[32,4,128]{2,1,0:T(4,128)(2,1)S(1)}, f32[32,512]{1,0:T(8,128)S(1)}, f32[32,512]{1,0:T(8,128)S(1)}, bf16[256,256]{1,0:T(8,128)(2,1)S(1)}) %tuple.18, (bf16[32,4,128]{2,1,0:T(4,128)(2,1)S(1)}, f32[32,512]{1,0:T(8,128)S(1)}, ...), branch_computations={%region_2.3_spmd, %region_3.4_spmd} | conditional | bytes 786440 | solution.py:307
  55.2 0.1 gate.3
  55.3 11.1 %all_to_all.29 = bf16[8,32,512]{2,1,0:T(8,128)(2,1)S(1)} all-to-all(bf16[8,32,512]{2,1,0:T(8,128)(2,1)S(1)} %gate.3), channel_id=1, replica_groups={{4,5,6,7,0,1,2,3},{12,13,14,15,8,9,10,11},{20,21,22,23,16,17,18,19},{28..., dimensions={0} | all-to-all | bytes 524288 | tf_op jit(solution)/shard_map/cond/branch_1_fun/all_to_all | solution.py:297
  66.4 1.0 %mix.3 = bf16[256,512]{1,0:T(8,128)(2,1)} custom-call(bf16[256,256]{1,0:T(8,128)(2,1)S(1)} %get-tuple-element.68.out_ref, bf16[256,512]{1,0:T(8,128)(2,1)S(1)} %bitcast.11), custom_call_target="tpu_custom_call" | custom-call | tf_op jit(solution)/shard_map/cond/branch_1_fun/mix/pallas_call | solution.py:298
Async XLA Ops:
  0.0 40.6 %copy-start.1 = (bf16[256,512]{1,0:T(8,128)(2,1)S(1)}, bf16[256,512]{1,0:T(8,128)(2,1)}, u32[]{:S(2)}) copy-start(bf16[256,512]{1,0:T(8,128)(2,1)} %constant.42.clone.back_lo) | copy-start | bytes 786436
  0.0 40.6 %copy-start.2 = (bf16[256,512]{1,0:T(8,128)(2,1)S(1)}, bf16[256,512]{1,0:T(8,128)(2,1)}, u32[]{:S(2)}) copy-start(bf16[256,512]{1,0:T(8,128)(2,1)} %constant.41.clone.back_hi) | copy-start | bytes 786436
  0.0 40.6 %copy-start.3 = (bf16[512,256]{1,0:T(8,128)(2,1)S(1)}, bf16[512,256]{1,0:T(8,128)(2,1)}, u32[]{:S(2)}) copy-start(bf16[512,256]{1,0:T(8,128)(2,1)} %constant.40.clone.fwd_lo) | copy-start | bytes 786436
  0.0 40.6 %copy-start.4 = (bf16[512,256]{1,0:T(8,128)(2,1)S(1)}, bf16[512,256]{1,0:T(8,128)(2,1)}, u32[]{:S(2)}) copy-start(bf16[512,256]{1,0:T(8,128)(2,1)} %constant.39.clone.fwd_hi) | copy-start | bytes 786436
  0.0 40.6 %copy-start.5 = (bf16[256,256]{1,0:T(8,128)(2,1)S(1)}, bf16[256,256]{1,0:T(8,128)(2,1)}, u32[]{:S(2)}) copy-start(bf16[256,256]{1,0:T(8,128)(2,1)} %constant.46.clone.out_lo) | copy-start | bytes 393220
  0.0 40.6 %copy-start.6 = (bf16[256,256]{1,0:T(8,128)(2,1)S(1)}, bf16[256,256]{1,0:T(8,128)(2,1)}, u32[]{:S(2)}) copy-start(bf16[256,256]{1,0:T(8,128)(2,1)} %constant.45.clone.out_hi) | copy-start | bytes 393220
  0.0 40.6 %copy-start.7 = (bf16[256,256]{1,0:T(8,128)(2,1)S(1)}, bf16[256,256]{1,0:T(8,128)(2,1)}, u32[]{:S(2)}) copy-start(bf16[256,256]{1,0:T(8,128)(2,1)} %constant.44.clone.in_lo) | copy-start | bytes 393220
  0.1 40.6 %copy-start.8 = (bf16[256,256]{1,0:T(8,128)(2,1)S(1)}, bf16[256,256]{1,0:T(8,128)(2,1)}, u32[]{:S(2)}) copy-start(bf16[256,256]{1,0:T(8,128)(2,1)} %constant.43.clone.in_hi) | copy-start | bytes 393220
  17.9 22.8 %copy-start = (f32[2,256,128]{2,1,0:T(8,128)S(1)}, f32[2,256,128]{2,1,0:T(8,128)}, u32[]{:S(2)}) copy-start(f32[2,256,128]{2,1,0:T(8,128)} %constant.47.clone.twist_ref) | copy-start | bytes 786436

commit v5 on v4

--- a/solution.py
+++ b/solution.py
@@ -23,7 +23,7 @@
 ]
 ORDER = HALVES[0] + HALVES[1]
 
-GROUP = [4, 5, 6, 7, 0, 1, 2, 3]
+GROUP = [5, 4, 6, 7, 0, 1, 2, 3]
 
 
 def split_table(table):

time: 67.6 us -> 66.4 us (0.982)
  blocking collectives: 63.6 us -> 62.4 us
where the time goes in v5:
time: 66.4 us; the launch traced here: 66.1 us
  blocking collectives  62.4 us (94%)
  Pallas kernels  3.54 us (5%)
    all_to_all x1, blocking collectives, shards(): lax.all_to_all(send, 'context', 0, 0, axis_index_groups=[ORDER], tiled=True)  22.3 us
    all_to_all x1, blocking collectives, begin(): lax.all_to_all(send, 'tensor', 0, 0, axis_index_groups=[GROUP], tiled=True)  16.3 us
    all_to_all x1, blocking collectives, shards(): lax.all_to_all(send, 'context', 0, 0, axis_index_groups=HALVES, tiled=True)  13.4 us
    all_to_all x1, blocking collectives, finish(): lax.all_to_all(send, 'tensor', 0, 0, axis_index_groups=[GROUP], tiled=True)  10.4 us

profile of v5, /device:TPU:1, one launch (start us, length us, event | category | flops | bytes accessed | tf_op | source)
XLA Modules:
  0.0 66.1 jit_solution(6182966614031459346)
XLA Ops:
  0.0 0.0 copy-start.1
  0.0 0.0 copy-start.2
  0.0 0.0 copy-start.3
  0.0 0.0 copy-start.4
  0.0 0.0 copy-start.5
  0.0 0.0 copy-start.6
  0.0 0.0 copy-start.7
  0.1 0.0 copy-start.8
  0.1 17.7 %conditional.2 = ((bf16[64,8,128]{2,1,0:T(8,128)(2,1)S(1)}, f32[32,512]{1,0:T(8,128)S(1)}, f32[32,512]{1,0:T(8,128)S(1)}, bf16[256,256]{1,0:T(8,128)(2,1)S(1)})) conditional(s32[]{:T(128)} %convert_element_type.4, (bf16[3,256,32]{1,2,0:T(8,128)(2,1)}, f32[32]{0:T(128)}, bf16[32,512]{1,0:T(8,128)(2,1)}, f32[32,512]{1,0:T(8,128)}, ...), branch_computations={%region_0.1_spmd, %region_1.2_spmd} | conditional | bytes 786440 | solution.py:265
  0.1 1.0 %spread.3 = (bf16[8,32,768]{2,1,0:T(8,128)(2,1)S(1)}, bf16[3,32,256]{2,1,0:T(8,128)(2,1)S(1)}, f32[32,512]{1,0:T(8,128)S(1)}, f32[1,32]{1,0:T(1,128)S(1)}, bf16[32,256]{1,0:T(8,128)(2,1)S(1)}) custom-call(bf16[32,512]{1,0:T(8,128)(2,1)} %get-tuple-element.54.sequence_ref, bf16[3,32,256]{2,1,0:T(8,128)(2,1)} %bitcast.13, ...), custom_call_target="tpu_custom_call" | custom-call | tf_op jit(solution)/shard_map/cond/branch_1_fun/spread/pallas_call | solution.py:237
  1.1 16.3 %all_to_all.27 = bf16[8,32,768]{2,1,0:T(8,128)(2,1)S(1)} all-to-all(bf16[8,32,768]{2,1,0:T(8,128)(2,1)S(1)} %get-tuple-element.59), channel_id=1, replica_groups={{5,4,6,7,0,1,2,3},{13,12,14,15,8,9,10,11},{21,20,22,23,16,17,18,19},{29..., dimensions={0} | all-to-all | bytes 786432 | tf_op jit(solution)/shard_map/cond/branch_1_fun/all_to_all | solution.py:247
  17.4 0.3 project.3
  17.8 0.0 copy-start
  17.8 22.3 %all_to_all.30.recv_ref = bf16[64,8,128]{2,1,0:T(8,128)(2,1)S(1)} all-to-all(bf16[64,8,128]{2,1,0:T(8,128)(2,1)S(1)} %get-tuple-element.76), channel_id=1, replica_groups={{336,344,352,360,368,376,320,328,464,472,480,488,496,504,448,456,80,88,..., dimensions={0} | all-to-all | bytes 262144 | tf_op jit(solution)/shard_map/all_to_all | solution.py:269
  40.0 0.0 copy-done.1
  40.1 0.0 copy-done.2
  40.1 0.0 copy-done.3
  40.1 0.0 copy-done.4
  40.1 0.0 copy-done.5
  40.1 0.0 copy-done.6
  40.1 0.0 copy-done.7
  40.1 0.0 copy-done.8
  40.1 0.0 copy-done
  40.1 1.2 %convolve.1 = bf16[32,4,128]{2,1,0:T(4,128)(2,1)S(1)} custom-call(bf16[64,8,128]{2,1,0:T(8,128)(2,1)S(1)} %all_to_all.30.recv_ref, bf16[512,256]{1,0:T(8,128)(2,1)S(1)} %copy-done.4, bf16[512,256]{1,0:T(8,128)(2,1)S(1)} %copy-done.3, bf16[256,512]{1,0:T(8,128)(2,1)S(1)} %copy-done.2, bf16[256,512]{1,0:T(8,128)(2,1)S(1)} %copy-done.1, ...), custom_call_target="tpu_custom_call" | custom-call | tf_op jit(solution)/shard_map/convolve/pallas_call | solution.py:272
  41.3 13.4 %all_to_all.31 = bf16[32,4,128]{2,1,0:T(4,128)(2,1)S(1)} all-to-all(bf16[32,4,128]{2,1,0:T(4,128)(2,1)S(1)} %convolve.1), channel_id=1, replica_groups={{336,344,352,360,368,376,320,328,464,472,480,488,496,504,448,456,80,88,..., dimensions={0} | all-to-all | bytes 65536 | tf_op jit(solution)/shard_map/all_to_all | solution.py:285
  54.7 11.5 %conditional.3 = (bf16[256,512]{1,0:T(8,128)(2,1)}) conditional(s32[]{:T(128)} %convert_element_type.4, (bf16[32,4,128]{2,1,0:T(4,128)(2,1)S(1)}, f32[32,512]{1,0:T(8,128)S(1)}, f32[32,512]{1,0:T(8,128)S(1)}, bf16[256,256]{1,0:T(8,128)(2,1)S(1)}) %tuple.18, (bf16[32,4,128]{2,1,0:T(4,128)(2,1)S(1)}, f32[32,512]{1,0:T(8,128)S(1)}, ...), branch_computations={%region_2.3_spmd, %region_3.4_spmd} | conditional | bytes 786440 | solution.py:307
  54.7 0.1 gate.3
  54.7 10.4 %all_to_all.29 = bf16[8,32,512]{2,1,0:T(8,128)(2,1)S(1)} all-to-all(bf16[8,32,512]{2,1,0:T(8,128)(2,1)S(1)} %gate.3), channel_id=1, replica_groups={{5,4,6,7,0,1,2,3},{13,12,14,15,8,9,10,11},{21,20,22,23,16,17,18,19},{29..., dimensions={0} | all-to-all | bytes 524288 | tf_op jit(solution)/shard_map/cond/branch_1_fun/all_to_all | solution.py:297
  65.2 1.0 %mix.3 = bf16[256,512]{1,0:T(8,128)(2,1)} custom-call(bf16[256,256]{1,0:T(8,128)(2,1)S(1)} %get-tuple-element.68.out_ref, bf16[256,512]{1,0:T(8,128)(2,1)S(1)} %bitcast.11), custom_call_target="tpu_custom_call" | custom-call | tf_op jit(solution)/shard_map/cond/branch_1_fun/mix/pallas_call | solution.py:298
Async XLA Ops:
  0.0 40.1 %copy-start.1 = (bf16[256,512]{1,0:T(8,128)(2,1)S(1)}, bf16[256,512]{1,0:T(8,128)(2,1)}, u32[]{:S(2)}) copy-start(bf16[256,512]{1,0:T(8,128)(2,1)} %constant.42.clone.back_lo) | copy-start | bytes 786436
  0.0 40.1 %copy-start.2 = (bf16[256,512]{1,0:T(8,128)(2,1)S(1)}, bf16[256,512]{1,0:T(8,128)(2,1)}, u32[]{:S(2)}) copy-start(bf16[256,512]{1,0:T(8,128)(2,1)} %constant.41.clone.back_hi) | copy-start | bytes 786436
  0.0 40.1 %copy-start.3 = (bf16[512,256]{1,0:T(8,128)(2,1)S(1)}, bf16[512,256]{1,0:T(8,128)(2,1)}, u32[]{:S(2)}) copy-start(bf16[512,256]{1,0:T(8,128)(2,1)} %constant.40.clone.fwd_lo) | copy-start | bytes 786436
  0.0 40.1 %copy-start.4 = (bf16[512,256]{1,0:T(8,128)(2,1)S(1)}, bf16[512,256]{1,0:T(8,128)(2,1)}, u32[]{:S(2)}) copy-start(bf16[512,256]{1,0:T(8,128)(2,1)} %constant.39.clone.fwd_hi) | copy-start | bytes 786436
  0.0 40.1 %copy-start.5 = (bf16[256,256]{1,0:T(8,128)(2,1)S(1)}, bf16[256,256]{1,0:T(8,128)(2,1)}, u32[]{:S(2)}) copy-start(bf16[256,256]{1,0:T(8,128)(2,1)} %constant.46.clone.out_lo) | copy-start | bytes 393220
  0.0 40.0 %copy-start.6 = (bf16[256,256]{1,0:T(8,128)(2,1)S(1)}, bf16[256,256]{1,0:T(8,128)(2,1)}, u32[]{:S(2)}) copy-start(bf16[256,256]{1,0:T(8,128)(2,1)} %constant.45.clone.out_hi) | copy-start | bytes 393220
  0.0 40.0 %copy-start.7 = (bf16[256,256]{1,0:T(8,128)(2,1)S(1)}, bf16[256,256]{1,0:T(8,128)(2,1)}, u32[]{:S(2)}) copy-start(bf16[256,256]{1,0:T(8,128)(2,1)} %constant.44.clone.in_lo) | copy-start | bytes 393220
  0.1 40.0 %copy-start.8 = (bf16[256,256]{1,0:T(8,128)(2,1)S(1)}, bf16[256,256]{1,0:T(8,128)(2,1)}, u32[]{:S(2)}) copy-start(bf16[256,256]{1,0:T(8,128)(2,1)} %constant.43.clone.in_hi) | copy-start | bytes 393220
  17.8 22.4 %copy-start = (f32[2,256,128]{2,1,0:T(8,128)S(1)}, f32[2,256,128]{2,1,0:T(8,128)}, u32[]{:S(2)}) copy-start(f32[2,256,128]{2,1,0:T(8,128)} %constant.47.clone.twist_ref) | copy-start | bytes 786436

commit v6 on v5

--- a/solution.py
+++ b/solution.py
@@ -19,9 +19,11 @@
 TURN = 2
 HALVES = [
     [(outer + TURN) % LINES * RING + inner for outer in range(LINES) for inner in ring]
-    for ring in ((10, 11, 12, 13, 14, 15, 8, 9), (6, 7, 5, 4, 3, 2, 1, 0))
+    for ring in ((11, 12, 13, 14, 15, 8, 9, 10), (6, 7, 5, 4, 3, 2, 1, 0))
 ]
 ORDER = HALVES[0] + HALVES[1]
+
+EARLY = 3
 
 GROUP = [5, 4, 6, 7, 0, 1, 2, 3]
 
@@ -224,7 +226,7 @@
     groups = lax.axis_size("tensor")
     ranks = lax.axis_size("context")
 
-    early = lax.axis_index("context") % RING < RING // 2
+    early = lax.axis_index("context") % RING < EARLY
 
     def begin(lanes):
         operands = [

time: 66.4 us -> 66.4 us (level)
  no operation moved by 1% of the time
where the time goes in v6:
time: 66.4 us; the launch traced here: 66.1 us
  blocking collectives  62.4 us (94%)
  Pallas kernels  3.54 us (5%)
    all_to_all x1, blocking collectives, shards(): lax.all_to_all(send, 'context', 0, 0, axis_index_groups=[ORDER], tiled=True)  22.2 us
    all_to_all x1, blocking collectives, begin(): lax.all_to_all(send, 'tensor', 0, 0, axis_index_groups=[GROUP], tiled=True)  16.3 us
    all_to_all x1, blocking collectives, shards(): lax.all_to_all(send, 'context', 0, 0, axis_index_groups=HALVES, tiled=True)  13.4 us
    all_to_all x1, blocking collectives, finish(): lax.all_to_all(send, 'tensor', 0, 0, axis_index_groups=[GROUP], tiled=True)  10.5 us

profile of v6, /device:TPU:1, one launch (start us, length us, event | category | flops | bytes accessed | tf_op | source)
XLA Modules:
  0.0 66.1 jit_solution(14238075050369154904)
XLA Ops:
  0.0 0.0 copy-start.1
  0.0 0.0 copy-start.2
  0.0 0.0 copy-start.3
  0.0 0.0 copy-start.4
  0.0 0.0 copy-start.5
  0.0 0.0 copy-start.6
  0.0 0.0 copy-start.7
  0.1 0.0 copy-start.8
  0.1 17.7 %conditional.2 = ((bf16[64,8,128]{2,1,0:T(8,128)(2,1)S(1)}, f32[32,512]{1,0:T(8,128)S(1)}, f32[32,512]{1,0:T(8,128)S(1)}, bf16[256,256]{1,0:T(8,128)(2,1)S(1)})) conditional(s32[]{:T(128)} %convert_element_type.4, (bf16[3,256,32]{1,2,0:T(8,128)(2,1)}, f32[32]{0:T(128)}, bf16[32,512]{1,0:T(8,128)(2,1)}, f32[32,512]{1,0:T(8,128)}, ...), branch_computations={%region_0.1_spmd, %region_1.2_spmd} | conditional | bytes 786440 | solution.py:267
  0.1 1.0 %spread.3 = (bf16[8,32,768]{2,1,0:T(8,128)(2,1)S(1)}, bf16[3,32,256]{2,1,0:T(8,128)(2,1)S(1)}, f32[32,512]{1,0:T(8,128)S(1)}, f32[1,32]{1,0:T(1,128)S(1)}, bf16[32,256]{1,0:T(8,128)(2,1)S(1)}) custom-call(bf16[32,512]{1,0:T(8,128)(2,1)} %get-tuple-element.54.sequence_ref, bf16[3,32,256]{2,1,0:T(8,128)(2,1)} %bitcast.13, ...), custom_call_target="tpu_custom_call" | custom-call | tf_op jit(solution)/shard_map/cond/branch_1_fun/spread/pallas_call | solution.py:239
  1.1 16.3 %all_to_all.27 = bf16[8,32,768]{2,1,0:T(8,128)(2,1)S(1)} all-to-all(bf16[8,32,768]{2,1,0:T(8,128)(2,1)S(1)} %get-tuple-element.59), channel_id=1, replica_groups={{5,4,6,7,0,1,2,3},{13,12,14,15,8,9,10,11},{21,20,22,23,16,17,18,19},{29..., dimensions={0} | all-to-all | bytes 786432 | tf_op jit(solution)/shard_map/cond/branch_1_fun/all_to_all | solution.py:249
  17.4 0.3 project.3
  17.8 0.0 copy-start
  17.8 22.2 %all_to_all.30.recv_ref = bf16[64,8,128]{2,1,0:T(8,128)(2,1)S(1)} all-to-all(bf16[64,8,128]{2,1,0:T(8,128)(2,1)S(1)} %get-tuple-element.76), channel_id=1, replica_groups={{344,352,360,368,376,320,328,336,472,480,488,496,504,448,456,464,88,96,..., dimensions={0} | all-to-all | bytes 262144 | tf_op jit(solution)/shard_map/all_to_all | solution.py:271
  40.0 0.0 copy-done.1
  40.0 0.0 copy-done.2
  40.0 0.0 copy-done.3
  40.0 0.0 copy-done.4
  40.0 0.0 copy-done.5
  40.0 0.0 copy-done.6
  40.0 0.0 copy-done.7
  40.1 0.0 copy-done.8
  40.1 0.0 copy-done
  40.1 1.2 %convolve.1 = bf16[32,4,128]{2,1,0:T(4,128)(2,1)S(1)} custom-call(bf16[64,8,128]{2,1,0:T(8,128)(2,1)S(1)} %all_to_all.30.recv_ref, bf16[512,256]{1,0:T(8,128)(2,1)S(1)} %copy-done.4, bf16[512,256]{1,0:T(8,128)(2,1)S(1)} %copy-done.3, bf16[256,512]{1,0:T(8,128)(2,1)S(1)} %copy-done.2, bf16[256,512]{1,0:T(8,128)(2,1)S(1)} %copy-done.1, ...), custom_call_target="tpu_custom_call" | custom-call | tf_op jit(solution)/shard_map/convolve/pallas_call | solution.py:274
  41.2 13.4 %all_to_all.31 = bf16[32,4,128]{2,1,0:T(4,128)(2,1)S(1)} all-to-all(bf16[32,4,128]{2,1,0:T(4,128)(2,1)S(1)} %convolve.1), channel_id=1, replica_groups={{344,352,360,368,376,320,328,336,472,480,488,496,504,448,456,464,88,96,..., dimensions={0} | all-to-all | bytes 65536 | tf_op jit(solution)/shard_map/all_to_all | solution.py:287
  54.6 11.5 %conditional.3 = (bf16[256,512]{1,0:T(8,128)(2,1)}) conditional(s32[]{:T(128)} %convert_element_type.4, (bf16[32,4,128]{2,1,0:T(4,128)(2,1)S(1)}, f32[32,512]{1,0:T(8,128)S(1)}, f32[32,512]{1,0:T(8,128)S(1)}, bf16[256,256]{1,0:T(8,128)(2,1)S(1)}) %tuple.18, (bf16[32,4,128]{2,1,0:T(4,128)(2,1)S(1)}, f32[32,512]{1,0:T(8,128)S(1)}, ...), branch_computations={%region_2.3_spmd, %region_3.4_spmd} | conditional | bytes 786440 | solution.py:309
  54.6 0.1 gate.3
  54.7 10.5 %all_to_all.29 = bf16[8,32,512]{2,1,0:T(8,128)(2,1)S(1)} all-to-all(bf16[8,32,512]{2,1,0:T(8,128)(2,1)S(1)} %gate.3), channel_id=1, replica_groups={{5,4,6,7,0,1,2,3},{13,12,14,15,8,9,10,11},{21,20,22,23,16,17,18,19},{29..., dimensions={0} | all-to-all | bytes 524288 | tf_op jit(solution)/shard_map/cond/branch_1_fun/all_to_all | solution.py:299
  65.2 1.0 %mix.3 = bf16[256,512]{1,0:T(8,128)(2,1)} custom-call(bf16[256,256]{1,0:T(8,128)(2,1)S(1)} %get-tuple-element.68.out_ref, bf16[256,512]{1,0:T(8,128)(2,1)S(1)} %bitcast.11), custom_call_target="tpu_custom_call" | custom-call | tf_op jit(solution)/shard_map/cond/branch_1_fun/mix/pallas_call | solution.py:300
Async XLA Ops:
  0.0 40.0 %copy-start.1 = (bf16[256,512]{1,0:T(8,128)(2,1)S(1)}, bf16[256,512]{1,0:T(8,128)(2,1)}, u32[]{:S(2)}) copy-start(bf16[256,512]{1,0:T(8,128)(2,1)} %constant.42.clone.back_lo) | copy-start | bytes 786436
  0.0 40.0 %copy-start.2 = (bf16[256,512]{1,0:T(8,128)(2,1)S(1)}, bf16[256,512]{1,0:T(8,128)(2,1)}, u32[]{:S(2)}) copy-start(bf16[256,512]{1,0:T(8,128)(2,1)} %constant.41.clone.back_hi) | copy-start | bytes 786436
  0.0 40.0 %copy-start.3 = (bf16[512,256]{1,0:T(8,128)(2,1)S(1)}, bf16[512,256]{1,0:T(8,128)(2,1)}, u32[]{:S(2)}) copy-start(bf16[512,256]{1,0:T(8,128)(2,1)} %constant.40.clone.fwd_lo) | copy-start | bytes 786436
  0.0 40.0 %copy-start.4 = (bf16[512,256]{1,0:T(8,128)(2,1)S(1)}, bf16[512,256]{1,0:T(8,128)(2,1)}, u32[]{:S(2)}) copy-start(bf16[512,256]{1,0:T(8,128)(2,1)} %constant.39.clone.fwd_hi) | copy-start | bytes 786436
  0.0 40.0 %copy-start.5 = (bf16[256,256]{1,0:T(8,128)(2,1)S(1)}, bf16[256,256]{1,0:T(8,128)(2,1)}, u32[]{:S(2)}) copy-start(bf16[256,256]{1,0:T(8,128)(2,1)} %constant.46.clone.out_lo) | copy-start | bytes 393220
  0.0 40.0 %copy-start.6 = (bf16[256,256]{1,0:T(8,128)(2,1)S(1)}, bf16[256,256]{1,0:T(8,128)(2,1)}, u32[]{:S(2)}) copy-start(bf16[256,256]{1,0:T(8,128)(2,1)} %constant.45.clone.out_hi) | copy-start | bytes 393220
  0.0 40.0 %copy-start.7 = (bf16[256,256]{1,0:T(8,128)(2,1)S(1)}, bf16[256,256]{1,0:T(8,128)(2,1)}, u32[]{:S(2)}) copy-start(bf16[256,256]{1,0:T(8,128)(2,1)} %constant.44.clone.in_lo) | copy-start | bytes 393220
  0.1 40.0 %copy-start.8 = (bf16[256,256]{1,0:T(8,128)(2,1)S(1)}, bf16[256,256]{1,0:T(8,128)(2,1)}, u32[]{:S(2)}) copy-start(bf16[256,256]{1,0:T(8,128)(2,1)} %constant.43.clone.in_hi) | copy-start | bytes 393220
  17.8 22.3 %copy-start = (f32[2,256,128]{2,1,0:T(8,128)S(1)}, f32[2,256,128]{2,1,0:T(8,128)}, u32[]{:S(2)}) copy-start(f32[2,256,128]{2,1,0:T(8,128)} %constant.47.clone.twist_ref) | copy-start | bytes 786436

commit v7 on v5

--- a/solution.py
+++ b/solution.py
@@ -121,14 +121,13 @@
         out_ref[...] = gathered_ref[:, tok_len:]
     else:
         out_ref[:channels] = own_ref[...]
-        out_ref[channels:] = jnp.zeros_like(out_ref[channels:])
     for piece in range(PIECE):
         cut = slice(piece * LANES, (piece + 1) * LANES)
-        for half in range(2):
-            span = slice(half * channels, (half + 1) * channels)
-            rows_ref[span, piece, :] = gated[:, cut]
-            rows_ref[span, PIECE + piece, :] = filter_ref[:, cut]
-    send_ref[...] = rows_ref[...].astype(jnp.bfloat16)
+        rows_ref[:, piece, :] = gated[:, cut]
+        rows_ref[:, PIECE + piece, :] = filter_ref[:, cut]
+    rows = rows_ref[...].astype(jnp.bfloat16)
+    for half in range(2):
+        send_ref[half * channels : (half + 1) * channels] = rows
 
 
 def convolve_kernel(
@@ -256,7 +255,7 @@
                 ),
                 in_specs=whole(5),
                 out_specs=tuple(whole(4)),
-                scratch_shapes=[pltpu.VMEM((ranks, 2 * PIECE, LANES), jnp.float32)],
+                scratch_shapes=[pltpu.VMEM((channels, 2 * PIECE, LANES), jnp.float32)],
                 compiler_params=pltpu.CompilerParams(vmem_limit_bytes=16 * 2**20),
                 name="project",
             )(*near(gathered.reshape(width, lanes), *local))

time: 66.4 us -> 66.3 us (level)
  no operation moved by 1% of the time
where the time goes in v7:
time: 66.3 us; the launch traced here: 66.1 us
  blocking collectives  62.4 us (94%)
  Pallas kernels  3.51 us (5%)
    all_to_all x1, blocking collectives, shards(): lax.all_to_all(send, 'context', 0, 0, axis_index_groups=[ORDER], tiled=True)  22.3 us
    all_to_all x1, blocking collectives, begin(): lax.all_to_all(send, 'tensor', 0, 0, axis_index_groups=[GROUP], tiled=True)  16.3 us
    all_to_all x1, blocking collectives, shards(): lax.all_to_all(send, 'context', 0, 0, axis_index_groups=HALVES, tiled=True)  13.4 us
    all_to_all x1, blocking collectives, finish(): lax.all_to_all(send, 'tensor', 0, 0, axis_index_groups=[GROUP], tiled=True)  10.4 us

profile of v7, /device:TPU:1, one launch (start us, length us, event | category | flops | bytes accessed | tf_op | source)
XLA Modules:
  0.0 66.1 jit_solution(10651805819842394710)
XLA Ops:
  0.0 0.0 copy-start.1
  0.0 0.0 copy-start.2
  0.0 0.0 copy-start.3
  0.0 0.0 copy-start.4
  0.0 0.0 copy-start.5
  0.0 0.0 copy-start.6
  0.0 0.0 copy-start.7
  0.1 0.0 copy-start.8
  0.1 17.6 %conditional.2 = ((bf16[64,8,128]{2,1,0:T(8,128)(2,1)S(1)}, f32[32,512]{1,0:T(8,128)S(1)}, f32[32,512]{1,0:T(8,128)S(1)}, bf16[256,256]{1,0:T(8,128)(2,1)S(1)})) conditional(s32[]{:T(128)} %convert_element_type.4, (bf16[3,256,32]{1,2,0:T(8,128)(2,1)}, f32[32]{0:T(128)}, bf16[32,512]{1,0:T(8,128)(2,1)}, f32[32,512]{1,0:T(8,128)}, ...), branch_computations={%region_0.1_spmd, %region_1.2_spmd} | conditional | bytes 786440 | solution.py:264
  0.1 1.0 %spread.3 = (bf16[8,32,768]{2,1,0:T(8,128)(2,1)S(1)}, bf16[3,32,256]{2,1,0:T(8,128)(2,1)S(1)}, f32[32,512]{1,0:T(8,128)S(1)}, f32[1,32]{1,0:T(1,128)S(1)}, bf16[32,256]{1,0:T(8,128)(2,1)S(1)}) custom-call(bf16[32,512]{1,0:T(8,128)(2,1)} %get-tuple-element.54.sequence_ref, bf16[3,32,256]{2,1,0:T(8,128)(2,1)} %bitcast.13, ...), custom_call_target="tpu_custom_call" | custom-call | tf_op jit(solution)/shard_map/cond/branch_1_fun/spread/pallas_call | solution.py:236
  1.1 16.3 %all_to_all.27 = bf16[8,32,768]{2,1,0:T(8,128)(2,1)S(1)} all-to-all(bf16[8,32,768]{2,1,0:T(8,128)(2,1)S(1)} %get-tuple-element.59), channel_id=1, replica_groups={{5,4,6,7,0,1,2,3},{13,12,14,15,8,9,10,11},{21,20,22,23,16,17,18,19},{29..., dimensions={0} | all-to-all | bytes 786432 | tf_op jit(solution)/shard_map/cond/branch_1_fun/all_to_all | solution.py:246
  17.4 0.3 project.3
  17.7 0.0 copy-start
  17.7 22.3 %all_to_all.30.recv_ref = bf16[64,8,128]{2,1,0:T(8,128)(2,1)S(1)} all-to-all(bf16[64,8,128]{2,1,0:T(8,128)(2,1)S(1)} %get-tuple-element.76), channel_id=1, replica_groups={{336,344,352,360,368,376,320,328,464,472,480,488,496,504,448,456,80,88,..., dimensions={0} | all-to-all | bytes 262144 | tf_op jit(solution)/shard_map/all_to_all | solution.py:268
  40.0 0.0 copy-done.1
  40.0 0.0 copy-done.2
  40.0 0.0 copy-done.3
  40.0 0.0 copy-done.4
  40.0 0.0 copy-done.5
  40.0 0.0 copy-done.6
  40.1 0.0 copy-done.7
  40.1 0.0 copy-done.8
  40.1 0.0 copy-done
  40.1 1.2 %convolve.1 = bf16[32,4,128]{2,1,0:T(4,128)(2,1)S(1)} custom-call(bf16[64,8,128]{2,1,0:T(8,128)(2,1)S(1)} %all_to_all.30.recv_ref, bf16[512,256]{1,0:T(8,128)(2,1)S(1)} %copy-done.4, bf16[512,256]{1,0:T(8,128)(2,1)S(1)} %copy-done.3, bf16[256,512]{1,0:T(8,128)(2,1)S(1)} %copy-done.2, bf16[256,512]{1,0:T(8,128)(2,1)S(1)} %copy-done.1, ...), custom_call_target="tpu_custom_call" | custom-call | tf_op jit(solution)/shard_map/convolve/pallas_call | solution.py:271
  41.3 13.4 %all_to_all.31 = bf16[32,4,128]{2,1,0:T(4,128)(2,1)S(1)} all-to-all(bf16[32,4,128]{2,1,0:T(4,128)(2,1)S(1)} %convolve.1), channel_id=1, replica_groups={{336,344,352,360,368,376,320,328,464,472,480,488,496,504,448,456,80,88,..., dimensions={0} | all-to-all | bytes 65536 | tf_op jit(solution)/shard_map/all_to_all | solution.py:284
  54.6 11.5 %conditional.3 = (bf16[256,512]{1,0:T(8,128)(2,1)}) conditional(s32[]{:T(128)} %convert_element_type.4, (bf16[32,4,128]{2,1,0:T(4,128)(2,1)S(1)}, f32[32,512]{1,0:T(8,128)S(1)}, f32[32,512]{1,0:T(8,128)S(1)}, bf16[256,256]{1,0:T(8,128)(2,1)S(1)}) %tuple.18, (bf16[32,4,128]{2,1,0:T(4,128)(2,1)S(1)}, f32[32,512]{1,0:T(8,128)S(1)}, ...), branch_computations={%region_2.3_spmd, %region_3.4_spmd} | conditional | bytes 786440 | solution.py:306
  54.6 0.1 gate.3
  54.7 10.4 %all_to_all.29 = bf16[8,32,512]{2,1,0:T(8,128)(2,1)S(1)} all-to-all(bf16[8,32,512]{2,1,0:T(8,128)(2,1)S(1)} %gate.3), channel_id=1, replica_groups={{5,4,6,7,0,1,2,3},{13,12,14,15,8,9,10,11},{21,20,22,23,16,17,18,19},{29..., dimensions={0} | all-to-all | bytes 524288 | tf_op jit(solution)/shard_map/cond/branch_1_fun/all_to_all | solution.py:296
  65.1 1.0 %mix.3 = bf16[256,512]{1,0:T(8,128)(2,1)} custom-call(bf16[256,256]{1,0:T(8,128)(2,1)S(1)} %get-tuple-element.68.out_ref, bf16[256,512]{1,0:T(8,128)(2,1)S(1)} %bitcast.11), custom_call_target="tpu_custom_call" | custom-call | tf_op jit(solution)/shard_map/cond/branch_1_fun/mix/pallas_call | solution.py:297
Async XLA Ops:
  0.0 40.0 %copy-start.1 = (bf16[256,512]{1,0:T(8,128)(2,1)S(1)}, bf16[256,512]{1,0:T(8,128)(2,1)}, u32[]{:S(2)}) copy-start(bf16[256,512]{1,0:T(8,128)(2,1)} %constant.42.clone.back_lo) | copy-start | bytes 786436
  0.0 40.0 %copy-start.2 = (bf16[256,512]{1,0:T(8,128)(2,1)S(1)}, bf16[256,512]{1,0:T(8,128)(2,1)}, u32[]{:S(2)}) copy-start(bf16[256,512]{1,0:T(8,128)(2,1)} %constant.41.clone.back_hi) | copy-start | bytes 786436
  0.0 40.0 %copy-start.3 = (bf16[512,256]{1,0:T(8,128)(2,1)S(1)}, bf16[512,256]{1,0:T(8,128)(2,1)}, u32[]{:S(2)}) copy-start(bf16[512,256]{1,0:T(8,128)(2,1)} %constant.40.clone.fwd_lo) | copy-start | bytes 786436
  0.0 40.0 %copy-start.4 = (bf16[512,256]{1,0:T(8,128)(2,1)S(1)}, bf16[512,256]{1,0:T(8,128)(2,1)}, u32[]{:S(2)}) copy-start(bf16[512,256]{1,0:T(8,128)(2,1)} %constant.39.clone.fwd_hi) | copy-start | bytes 786436
  0.0 40.0 %copy-start.5 = (bf16[256,256]{1,0:T(8,128)(2,1)S(1)}, bf16[256,256]{1,0:T(8,128)(2,1)}, u32[]{:S(2)}) copy-start(bf16[256,256]{1,0:T(8,128)(2,1)} %constant.46.clone.out_lo) | copy-start | bytes 393220
  0.0 40.0 %copy-start.6 = (bf16[256,256]{1,0:T(8,128)(2,1)S(1)}, bf16[256,256]{1,0:T(8,128)(2,1)}, u32[]{:S(2)}) copy-start(bf16[256,256]{1,0:T(8,128)(2,1)} %constant.45.clone.out_hi) | copy-start | bytes 393220
  0.0 40.0 %copy-start.7 = (bf16[256,256]{1,0:T(8,128)(2,1)S(1)}, bf16[256,256]{1,0:T(8,128)(2,1)}, u32[]{:S(2)}) copy-start(bf16[256,256]{1,0:T(8,128)(2,1)} %constant.44.clone.in_lo) | copy-start | bytes 393220
  0.1 40.0 %copy-start.8 = (bf16[256,256]{1,0:T(8,128)(2,1)S(1)}, bf16[256,256]{1,0:T(8,128)(2,1)}, u32[]{:S(2)}) copy-start(bf16[256,256]{1,0:T(8,128)(2,1)} %constant.43.clone.in_hi) | copy-start | bytes 393220
  17.7 22.4 %copy-start = (f32[2,256,128]{2,1,0:T(8,128)S(1)}, f32[2,256,128]{2,1,0:T(8,128)}, u32[]{:S(2)}) copy-start(f32[2,256,128]{2,1,0:T(8,128)} %constant.47.clone.twist_ref) | copy-start | bytes 786436

commit v8 on v7

--- a/solution.py
+++ b/solution.py
@@ -21,7 +21,7 @@
     [(outer + TURN) % LINES * RING + inner for outer in range(LINES) for inner in ring]
     for ring in ((10, 11, 12, 13, 14, 15, 8, 9), (6, 7, 5, 4, 3, 2, 1, 0))
 ]
-ORDER = HALVES[0] + HALVES[1]
+ORDER = HALVES[0][:1] + HALVES[1] + HALVES[0][1:]
 
 GROUP = [5, 4, 6, 7, 0, 1, 2, 3]
 
@@ -126,8 +126,9 @@
         rows_ref[:, piece, :] = gated[:, cut]
         rows_ref[:, PIECE + piece, :] = filter_ref[:, cut]
     rows = rows_ref[...].astype(jnp.bfloat16)
-    for half in range(2):
-        send_ref[half * channels : (half + 1) * channels] = rows
+    send_ref[:1] = rows[:1]
+    send_ref[1 : channels + 1] = rows
+    send_ref[channels + 1 :] = rows[1:]
 
 
 def convolve_kernel(

time: 66.3 us -> 66.2 us (level)
    all_to_all x1, blocking collectives: 10.4 us -> 11.9 us  [finish(): lax.all_to_all(send, 'tensor', 0, 0, axis_index_groups=[GROUP], tiled=True)]
    all_to_all x1, blocking collectives: 22.3 us -> 20.9 us  [shards(): lax.all_to_all(send, 'context', 0, 0, axis_index_groups=[ORDER], tiled=True)]
where the time goes in v8:
time: 66.2 us; the launch traced here: 66 us
  blocking collectives  62.3 us (94%)
  Pallas kernels  3.5 us (5%)
    all_to_all x1, blocking collectives, shards(): lax.all_to_all(send, 'context', 0, 0, axis_index_groups=[ORDER], tiled=True)  20.9 us
    all_to_all x1, blocking collectives, begin(): lax.all_to_all(send, 'tensor', 0, 0, axis_index_groups=[GROUP], tiled=True)  16.3 us
    all_to_all x1, blocking collectives, shards(): lax.all_to_all(send, 'context', 0, 0, axis_index_groups=HALVES, tiled=True)  13.1 us
    all_to_all x1, blocking collectives, finish(): lax.all_to_all(send, 'tensor', 0, 0, axis_index_groups=[GROUP], tiled=True)  11.9 us

profile of v8, /device:TPU:1, one launch (start us, length us, event | category | flops | bytes accessed | tf_op | source)
XLA Modules:
  0.0 66.0 jit_solution(9404467390148426814)
XLA Ops:
  0.0 0.0 copy-start.1
  0.0 0.0 copy-start.2
  0.0 0.0 copy-start.3
  0.0 0.0 copy-start.4
  0.0 0.0 copy-start.5
  0.0 0.0 copy-start.6
  0.0 0.0 copy-start.7
  0.1 0.0 copy-start.8
  0.1 17.7 %conditional.2 = ((bf16[64,8,128]{2,1,0:T(8,128)(2,1)S(1)}, f32[32,512]{1,0:T(8,128)S(1)}, f32[32,512]{1,0:T(8,128)S(1)}, bf16[256,256]{1,0:T(8,128)(2,1)S(1)})) conditional(s32[]{:T(128)} %convert_element_type.4, (bf16[3,256,32]{1,2,0:T(8,128)(2,1)}, f32[32]{0:T(128)}, bf16[32,512]{1,0:T(8,128)(2,1)}, f32[32,512]{1,0:T(8,128)}, ...), branch_computations={%region_0.1_spmd, %region_1.2_spmd} | conditional | bytes 786440 | solution.py:265
  0.1 1.0 %spread.3 = (bf16[8,32,768]{2,1,0:T(8,128)(2,1)S(1)}, bf16[3,32,256]{2,1,0:T(8,128)(2,1)S(1)}, f32[32,512]{1,0:T(8,128)S(1)}, f32[1,32]{1,0:T(1,128)S(1)}, bf16[32,256]{1,0:T(8,128)(2,1)S(1)}) custom-call(bf16[32,512]{1,0:T(8,128)(2,1)} %get-tuple-element.54.sequence_ref, bf16[3,32,256]{2,1,0:T(8,128)(2,1)} %bitcast.13, ...), custom_call_target="tpu_custom_call" | custom-call | tf_op jit(solution)/shard_map/cond/branch_1_fun/spread/pallas_call | solution.py:237
  1.1 16.3 %all_to_all.27 = bf16[8,32,768]{2,1,0:T(8,128)(2,1)S(1)} all-to-all(bf16[8,32,768]{2,1,0:T(8,128)(2,1)S(1)} %get-tuple-element.59), channel_id=1, replica_groups={{5,4,6,7,0,1,2,3},{13,12,14,15,8,9,10,11},{21,20,22,23,16,17,18,19},{29..., dimensions={0} | all-to-all | bytes 786432 | tf_op jit(solution)/shard_map/cond/branch_1_fun/all_to_all | solution.py:247
  17.4 0.3 project.3
  17.7 0.0 copy-start
  17.7 20.9 %all_to_all.30.recv_ref = bf16[64,8,128]{2,1,0:T(8,128)(2,1)S(1)} all-to-all(bf16[64,8,128]{2,1,0:T(8,128)(2,1)S(1)} %get-tuple-element.76), channel_id=1, replica_groups={{336,304,312,296,288,280,272,264,256,432,440,424,416,408,400,392,384,48..., dimensions={0} | all-to-all | bytes 262144 | tf_op jit(solution)/shard_map/all_to_all | solution.py:269
  38.7 0.0 copy-done.1
  38.7 0.0 copy-done.2
  38.7 0.0 copy-done.3
  38.7 0.0 copy-done.4
  38.7 0.0 copy-done.5
  38.7 0.0 copy-done.6
  38.7 0.0 copy-done.7
  38.7 0.0 copy-done.8
  38.7 0.0 copy-done
  38.8 1.2 %convolve.1 = bf16[32,4,128]{2,1,0:T(4,128)(2,1)S(1)} custom-call(bf16[64,8,128]{2,1,0:T(8,128)(2,1)S(1)} %all_to_all.30.recv_ref, bf16[512,256]{1,0:T(8,128)(2,1)S(1)} %copy-done.4, bf16[512,256]{1,0:T(8,128)(2,1)S(1)} %copy-done.3, bf16[256,512]{1,0:T(8,128)(2,1)S(1)} %copy-done.2, bf16[256,512]{1,0:T(8,128)(2,1)S(1)} %copy-done.1, ...), custom_call_target="tpu_custom_call" | custom-call | tf_op jit(solution)/shard_map/convolve/pallas_call | solution.py:272
  39.9 13.1 %all_to_all.31 = bf16[32,4,128]{2,1,0:T(4,128)(2,1)S(1)} all-to-all(bf16[32,4,128]{2,1,0:T(4,128)(2,1)S(1)} %convolve.1), channel_id=1, replica_groups={{336,344,352,360,368,376,320,328,464,472,480,488,496,504,448,456,80,88,..., dimensions={0} | all-to-all | bytes 65536 | tf_op jit(solution)/shard_map/all_to_all | solution.py:285
  53.0 12.9 %conditional.3 = (bf16[256,512]{1,0:T(8,128)(2,1)}) conditional(s32[]{:T(128)} %convert_element_type.4, (bf16[32,4,128]{2,1,0:T(4,128)(2,1)S(1)}, f32[32,512]{1,0:T(8,128)S(1)}, f32[32,512]{1,0:T(8,128)S(1)}, bf16[256,256]{1,0:T(8,128)(2,1)S(1)}) %tuple.18, (bf16[32,4,128]{2,1,0:T(4,128)(2,1)S(1)}, f32[32,512]{1,0:T(8,128)S(1)}, ...), branch_computations={%region_2.3_spmd, %region_3.4_spmd} | conditional | bytes 786440 | solution.py:307
  53.0 0.1 gate.3
  53.1 11.9 %all_to_all.29 = bf16[8,32,512]{2,1,0:T(8,128)(2,1)S(1)} all-to-all(bf16[8,32,512]{2,1,0:T(8,128)(2,1)S(1)} %gate.3), channel_id=1, replica_groups={{5,4,6,7,0,1,2,3},{13,12,14,15,8,9,10,11},{21,20,22,23,16,17,18,19},{29..., dimensions={0} | all-to-all | bytes 524288 | tf_op jit(solution)/shard_map/cond/branch_1_fun/all_to_all | solution.py:297
  65.0 1.0 %mix.3 = bf16[256,512]{1,0:T(8,128)(2,1)} custom-call(bf16[256,256]{1,0:T(8,128)(2,1)S(1)} %get-tuple-element.68.out_ref, bf16[256,512]{1,0:T(8,128)(2,1)S(1)} %bitcast.11), custom_call_target="tpu_custom_call" | custom-call | tf_op jit(solution)/shard_map/cond/branch_1_fun/mix/pallas_call | solution.py:298
Async XLA Ops:
  0.0 38.7 %copy-start.1 = (bf16[256,512]{1,0:T(8,128)(2,1)S(1)}, bf16[256,512]{1,0:T(8,128)(2,1)}, u32[]{:S(2)}) copy-start(bf16[256,512]{1,0:T(8,128)(2,1)} %constant.42.clone.back_lo) | copy-start | bytes 786436
  0.0 38.7 %copy-start.2 = (bf16[256,512]{1,0:T(8,128)(2,1)S(1)}, bf16[256,512]{1,0:T(8,128)(2,1)}, u32[]{:S(2)}) copy-start(bf16[256,512]{1,0:T(8,128)(2,1)} %constant.41.clone.back_hi) | copy-start | bytes 786436
  0.0 38.7 %copy-start.3 = (bf16[512,256]{1,0:T(8,128)(2,1)S(1)}, bf16[512,256]{1,0:T(8,128)(2,1)}, u32[]{:S(2)}) copy-start(bf16[512,256]{1,0:T(8,128)(2,1)} %constant.40.clone.fwd_lo) | copy-start | bytes 786436
  0.0 38.7 %copy-start.4 = (bf16[512,256]{1,0:T(8,128)(2,1)S(1)}, bf16[512,256]{1,0:T(8,128)(2,1)}, u32[]{:S(2)}) copy-start(bf16[512,256]{1,0:T(8,128)(2,1)} %constant.39.clone.fwd_hi) | copy-start | bytes 786436
  0.0 38.7 %copy-start.5 = (bf16[256,256]{1,0:T(8,128)(2,1)S(1)}, bf16[256,256]{1,0:T(8,128)(2,1)}, u32[]{:S(2)}) copy-start(bf16[256,256]{1,0:T(8,128)(2,1)} %constant.46.clone.out_lo) | copy-start | bytes 393220
  0.0 38.7 %copy-start.6 = (bf16[256,256]{1,0:T(8,128)(2,1)S(1)}, bf16[256,256]{1,0:T(8,128)(2,1)}, u32[]{:S(2)}) copy-start(bf16[256,256]{1,0:T(8,128)(2,1)} %constant.45.clone.out_hi) | copy-start | bytes 393220
  0.0 38.7 %copy-start.7 = (bf16[256,256]{1,0:T(8,128)(2,1)S(1)}, bf16[256,256]{1,0:T(8,128)(2,1)}, u32[]{:S(2)}) copy-start(bf16[256,256]{1,0:T(8,128)(2,1)} %constant.44.clone.in_lo) | copy-start | bytes 393220
  0.1 38.7 %copy-start.8 = (bf16[256,256]{1,0:T(8,128)(2,1)S(1)}, bf16[256,256]{1,0:T(8,128)(2,1)}, u32[]{:S(2)}) copy-start(bf16[256,256]{1,0:T(8,128)(2,1)} %constant.43.clone.in_hi) | copy-start | bytes 393220
  17.7 21.0 %copy-start = (f32[2,256,128]{2,1,0:T(8,128)S(1)}, f32[2,256,128]{2,1,0:T(8,128)}, u32[]{:S(2)}) copy-start(f32[2,256,128]{2,1,0:T(8,128)} %constant.47.clone.twist_ref) | copy-start | bytes 786436

commit v9 on v7

--- a/solution.py
+++ b/solution.py
@@ -19,9 +19,11 @@
 TURN = 2
 HALVES = [
     [(outer + TURN) % LINES * RING + inner for outer in range(LINES) for inner in ring]
-    for ring in ((10, 11, 12, 13, 14, 15, 8, 9), (6, 7, 5, 4, 3, 2, 1, 0))
+    for ring in ((11, 12, 13, 14, 15, 8, 9, 10), (6, 7, 5, 4, 3, 2, 1, 0))
 ]
 ORDER = HALVES[0] + HALVES[1]
+
+EARLY = 3
 
 GROUP = [5, 4, 6, 7, 0, 1, 2, 3]
 
@@ -223,7 +225,7 @@
     groups = lax.axis_size("tensor")
     ranks = lax.axis_size("context")
 
-    early = lax.axis_index("context") % RING < RING // 2
+    early = lax.axis_index("context") % RING < EARLY
 
     def begin(lanes):
         operands = [

time: 66.3 us -> 66.4 us (level)
  no operation moved by 1% of the time
where the time goes in v9:
time: 66.4 us; the launch traced here: 66.1 us
  blocking collectives  62.4 us (94%)
  Pallas kernels  3.51 us (5%)
    all_to_all x1, blocking collectives, shards(): lax.all_to_all(send, 'context', 0, 0, axis_index_groups=[ORDER], tiled=True)  22.2 us
    all_to_all x1, blocking collectives, begin(): lax.all_to_all(send, 'tensor', 0, 0, axis_index_groups=[GROUP], tiled=True)  16.3 us
    all_to_all x1, blocking collectives, shards(): lax.all_to_all(send, 'context', 0, 0, axis_index_groups=HALVES, tiled=True)  13.4 us
    all_to_all x1, blocking collectives, finish(): lax.all_to_all(send, 'tensor', 0, 0, axis_index_groups=[GROUP], tiled=True)  10.5 us

profile of v9, /device:TPU:1, one launch (start us, length us, event | category | flops | bytes accessed | tf_op | source)
XLA Modules:
  0.0 66.1 jit_solution(1862092913382923781)
XLA Ops:
  0.0 0.0 copy-start.1
  0.0 0.0 copy-start.2
  0.0 0.0 copy-start.3
  0.0 0.0 copy-start.4
  0.0 0.0 copy-start.5
  0.0 0.0 copy-start.6
  0.0 0.0 copy-start.7
  0.1 0.0 copy-start.8
  0.1 17.6 %conditional.2 = ((bf16[64,8,128]{2,1,0:T(8,128)(2,1)S(1)}, f32[32,512]{1,0:T(8,128)S(1)}, f32[32,512]{1,0:T(8,128)S(1)}, bf16[256,256]{1,0:T(8,128)(2,1)S(1)})) conditional(s32[]{:T(128)} %convert_element_type.4, (bf16[3,256,32]{1,2,0:T(8,128)(2,1)}, f32[32]{0:T(128)}, bf16[32,512]{1,0:T(8,128)(2,1)}, f32[32,512]{1,0:T(8,128)}, ...), branch_computations={%region_0.1_spmd, %region_1.2_spmd} | conditional | bytes 786440 | solution.py:266
  0.1 1.0 %spread.3 = (bf16[8,32,768]{2,1,0:T(8,128)(2,1)S(1)}, bf16[3,32,256]{2,1,0:T(8,128)(2,1)S(1)}, f32[32,512]{1,0:T(8,128)S(1)}, f32[1,32]{1,0:T(1,128)S(1)}, bf16[32,256]{1,0:T(8,128)(2,1)S(1)}) custom-call(bf16[32,512]{1,0:T(8,128)(2,1)} %get-tuple-element.54.sequence_ref, bf16[3,32,256]{2,1,0:T(8,128)(2,1)} %bitcast.13, ...), custom_call_target="tpu_custom_call" | custom-call | tf_op jit(solution)/shard_map/cond/branch_1_fun/spread/pallas_call | solution.py:238
  1.1 16.3 %all_to_all.27 = bf16[8,32,768]{2,1,0:T(8,128)(2,1)S(1)} all-to-all(bf16[8,32,768]{2,1,0:T(8,128)(2,1)S(1)} %get-tuple-element.59), channel_id=1, replica_groups={{5,4,6,7,0,1,2,3},{13,12,14,15,8,9,10,11},{21,20,22,23,16,17,18,19},{29..., dimensions={0} | all-to-all | bytes 786432 | tf_op jit(solution)/shard_map/cond/branch_1_fun/all_to_all | solution.py:248
  17.4 0.3 project.3
  17.7 0.0 copy-start
  17.7 22.2 %all_to_all.30.recv_ref = bf16[64,8,128]{2,1,0:T(8,128)(2,1)S(1)} all-to-all(bf16[64,8,128]{2,1,0:T(8,128)(2,1)S(1)} %get-tuple-element.76), channel_id=1, replica_groups={{344,352,360,368,376,320,328,336,472,480,488,496,504,448,456,464,88,96,..., dimensions={0} | all-to-all | bytes 262144 | tf_op jit(solution)/shard_map/all_to_all | solution.py:270
  40.0 0.0 copy-done.1
  40.0 0.0 copy-done.2
  40.0 0.0 copy-done.3
  40.0 0.0 copy-done.4
  40.0 0.0 copy-done.5
  40.0 0.0 copy-done.6
  40.0 0.0 copy-done.7
  40.0 0.0 copy-done.8
  40.0 0.0 copy-done
  40.0 1.2 %convolve.1 = bf16[32,4,128]{2,1,0:T(4,128)(2,1)S(1)} custom-call(bf16[64,8,128]{2,1,0:T(8,128)(2,1)S(1)} %all_to_all.30.recv_ref, bf16[512,256]{1,0:T(8,128)(2,1)S(1)} %copy-done.4, bf16[512,256]{1,0:T(8,128)(2,1)S(1)} %copy-done.3, bf16[256,512]{1,0:T(8,128)(2,1)S(1)} %copy-done.2, bf16[256,512]{1,0:T(8,128)(2,1)S(1)} %copy-done.1, ...), custom_call_target="tpu_custom_call" | custom-call | tf_op jit(solution)/shard_map/convolve/pallas_call | solution.py:273
  41.2 13.4 %all_to_all.31 = bf16[32,4,128]{2,1,0:T(4,128)(2,1)S(1)} all-to-all(bf16[32,4,128]{2,1,0:T(4,128)(2,1)S(1)} %convolve.1), channel_id=1, replica_groups={{344,352,360,368,376,320,328,336,472,480,488,496,504,448,456,464,88,96,..., dimensions={0} | all-to-all | bytes 65536 | tf_op jit(solution)/shard_map/all_to_all | solution.py:286
  54.6 11.5 %conditional.3 = (bf16[256,512]{1,0:T(8,128)(2,1)}) conditional(s32[]{:T(128)} %convert_element_type.4, (bf16[32,4,128]{2,1,0:T(4,128)(2,1)S(1)}, f32[32,512]{1,0:T(8,128)S(1)}, f32[32,512]{1,0:T(8,128)S(1)}, bf16[256,256]{1,0:T(8,128)(2,1)S(1)}) %tuple.18, (bf16[32,4,128]{2,1,0:T(4,128)(2,1)S(1)}, f32[32,512]{1,0:T(8,128)S(1)}, ...), branch_computations={%region_2.3_spmd, %region_3.4_spmd} | conditional | bytes 786440 | solution.py:308
  54.6 0.1 gate.3
  54.6 10.5 %all_to_all.29 = bf16[8,32,512]{2,1,0:T(8,128)(2,1)S(1)} all-to-all(bf16[8,32,512]{2,1,0:T(8,128)(2,1)S(1)} %gate.3), channel_id=1, replica_groups={{5,4,6,7,0,1,2,3},{13,12,14,15,8,9,10,11},{21,20,22,23,16,17,18,19},{29..., dimensions={0} | all-to-all | bytes 524288 | tf_op jit(solution)/shard_map/cond/branch_1_fun/all_to_all | solution.py:298
  65.1 1.0 %mix.3 = bf16[256,512]{1,0:T(8,128)(2,1)} custom-call(bf16[256,256]{1,0:T(8,128)(2,1)S(1)} %get-tuple-element.68.out_ref, bf16[256,512]{1,0:T(8,128)(2,1)S(1)} %bitcast.11), custom_call_target="tpu_custom_call" | custom-call | tf_op jit(solution)/shard_map/cond/branch_1_fun/mix/pallas_call | solution.py:299
Async XLA Ops:
  0.0 40.0 %copy-start.1 = (bf16[256,512]{1,0:T(8,128)(2,1)S(1)}, bf16[256,512]{1,0:T(8,128)(2,1)}, u32[]{:S(2)}) copy-start(bf16[256,512]{1,0:T(8,128)(2,1)} %constant.42.clone.back_lo) | copy-start | bytes 786436
  0.0 40.0 %copy-start.2 = (bf16[256,512]{1,0:T(8,128)(2,1)S(1)}, bf16[256,512]{1,0:T(8,128)(2,1)}, u32[]{:S(2)}) copy-start(bf16[256,512]{1,0:T(8,128)(2,1)} %constant.41.clone.back_hi) | copy-start | bytes 786436
  0.0 40.0 %copy-start.3 = (bf16[512,256]{1,0:T(8,128)(2,1)S(1)}, bf16[512,256]{1,0:T(8,128)(2,1)}, u32[]{:S(2)}) copy-start(bf16[512,256]{1,0:T(8,128)(2,1)} %constant.40.clone.fwd_lo) | copy-start | bytes 786436
  0.0 40.0 %copy-start.4 = (bf16[512,256]{1,0:T(8,128)(2,1)S(1)}, bf16[512,256]{1,0:T(8,128)(2,1)}, u32[]{:S(2)}) copy-start(bf16[512,256]{1,0:T(8,128)(2,1)} %constant.39.clone.fwd_hi) | copy-start | bytes 786436
  0.0 40.0 %copy-start.5 = (bf16[256,256]{1,0:T(8,128)(2,1)S(1)}, bf16[256,256]{1,0:T(8,128)(2,1)}, u32[]{:S(2)}) copy-start(bf16[256,256]{1,0:T(8,128)(2,1)} %constant.46.clone.out_lo) | copy-start | bytes 393220
  0.0 40.0 %copy-start.6 = (bf16[256,256]{1,0:T(8,128)(2,1)S(1)}, bf16[256,256]{1,0:T(8,128)(2,1)}, u32[]{:S(2)}) copy-start(bf16[256,256]{1,0:T(8,128)(2,1)} %constant.45.clone.out_hi) | copy-start | bytes 393220
  0.0 40.0 %copy-start.7 = (bf16[256,256]{1,0:T(8,128)(2,1)S(1)}, bf16[256,256]{1,0:T(8,128)(2,1)}, u32[]{:S(2)}) copy-start(bf16[256,256]{1,0:T(8,128)(2,1)} %constant.44.clone.in_lo) | copy-start | bytes 393220
  0.1 40.0 %copy-start.8 = (bf16[256,256]{1,0:T(8,128)(2,1)S(1)}, bf16[256,256]{1,0:T(8,128)(2,1)}, u32[]{:S(2)}) copy-start(bf16[256,256]{1,0:T(8,128)(2,1)} %constant.43.clone.in_hi) | copy-start | bytes 393220
  17.7 22.3 %copy-start = (f32[2,256,128]{2,1,0:T(8,128)S(1)}, f32[2,256,128]{2,1,0:T(8,128)}, u32[]{:S(2)}) copy-start(f32[2,256,128]{2,1,0:T(8,128)} %constant.47.clone.twist_ref) | copy-start | bytes 786436

commit v10 on v5

--- a/solution.py
+++ b/solution.py
@@ -19,7 +19,7 @@
 TURN = 2
 HALVES = [
     [(outer + TURN) % LINES * RING + inner for outer in range(LINES) for inner in ring]
-    for ring in ((10, 11, 12, 13, 14, 15, 8, 9), (6, 7, 5, 4, 3, 2, 1, 0))
+    for ring in ((10, 11, 12, 13, 14, 15, 8, 9), (6, 5, 4, 7, 3, 2, 1, 0))
 ]
 ORDER = HALVES[0] + HALVES[1]
 

time: 66.4 us -> 66.5 us (level)
  no operation moved by 1% of the time
where the time goes in v10:
time: 66.5 us; the launch traced here: 66.2 us
  blocking collectives  62.5 us (94%)
  Pallas kernels  3.54 us (5%)
    all_to_all x1, blocking collectives, shards(): lax.all_to_all(send, 'context', 0, 0, axis_index_groups=[ORDER], tiled=True)  22.1 us
    all_to_all x1, blocking collectives, begin(): lax.all_to_all(send, 'tensor', 0, 0, axis_index_groups=[GROUP], tiled=True)  16.3 us
    all_to_all x1, blocking collectives, shards(): lax.all_to_all(send, 'context', 0, 0, axis_index_groups=HALVES, tiled=True)  13.4 us
    all_to_all x1, blocking collectives, finish(): lax.all_to_all(send, 'tensor', 0, 0, axis_index_groups=[GROUP], tiled=True)  10.6 us

profile of v10, /device:TPU:1, one launch (start us, length us, event | category | flops | bytes accessed | tf_op | source)
XLA Modules:
  0.0 66.2 jit_solution(4085833895675407680)
XLA Ops:
  0.0 0.0 copy-start.1
  0.0 0.0 copy-start.2
  0.0 0.0 copy-start.3
  0.0 0.0 copy-start.4
  0.0 0.0 copy-start.5
  0.0 0.0 copy-start.6
  0.0 0.0 copy-start.7
  0.1 0.0 copy-start.8
  0.1 17.7 %conditional.2 = ((bf16[64,8,128]{2,1,0:T(8,128)(2,1)S(1)}, f32[32,512]{1,0:T(8,128)S(1)}, f32[32,512]{1,0:T(8,128)S(1)}, bf16[256,256]{1,0:T(8,128)(2,1)S(1)})) conditional(s32[]{:T(128)} %convert_element_type.4, (bf16[3,256,32]{1,2,0:T(8,128)(2,1)}, f32[32]{0:T(128)}, bf16[32,512]{1,0:T(8,128)(2,1)}, f32[32,512]{1,0:T(8,128)}, ...), branch_computations={%region_0.1_spmd, %region_1.2_spmd} | conditional | bytes 786440 | solution.py:265
  0.1 1.0 %spread.3 = (bf16[8,32,768]{2,1,0:T(8,128)(2,1)S(1)}, bf16[3,32,256]{2,1,0:T(8,128)(2,1)S(1)}, f32[32,512]{1,0:T(8,128)S(1)}, f32[1,32]{1,0:T(1,128)S(1)}, bf16[32,256]{1,0:T(8,128)(2,1)S(1)}) custom-call(bf16[32,512]{1,0:T(8,128)(2,1)} %get-tuple-element.54.sequence_ref, bf16[3,32,256]{2,1,0:T(8,128)(2,1)} %bitcast.13, ...), custom_call_target="tpu_custom_call" | custom-call | tf_op jit(solution)/shard_map/cond/branch_1_fun/spread/pallas_call | solution.py:237
  1.1 16.3 %all_to_all.27 = bf16[8,32,768]{2,1,0:T(8,128)(2,1)S(1)} all-to-all(bf16[8,32,768]{2,1,0:T(8,128)(2,1)S(1)} %get-tuple-element.59), channel_id=1, replica_groups={{5,4,6,7,0,1,2,3},{13,12,14,15,8,9,10,11},{21,20,22,23,16,17,18,19},{29..., dimensions={0} | all-to-all | bytes 786432 | tf_op jit(solution)/shard_map/cond/branch_1_fun/all_to_all | solution.py:247
  17.4 0.3 project.3
  17.8 0.0 copy-start
  17.8 22.1 %all_to_all.30.recv_ref = bf16[64,8,128]{2,1,0:T(8,128)(2,1)S(1)} all-to-all(bf16[64,8,128]{2,1,0:T(8,128)(2,1)S(1)} %get-tuple-element.76), channel_id=1, replica_groups={{336,344,352,360,368,376,320,328,464,472,480,488,496,504,448,456,80,88,..., dimensions={0} | all-to-all | bytes 262144 | tf_op jit(solution)/shard_map/all_to_all | solution.py:269
  39.8 0.0 copy-done.1
  39.8 0.0 copy-done.2
  39.8 0.0 copy-done.3
  39.9 0.0 copy-done.4
  39.9 0.0 copy-done.5
  39.9 0.0 copy-done.6
  39.9 0.0 copy-done.7
  39.9 0.0 copy-done.8
  39.9 0.0 copy-done
  39.9 1.2 %convolve.1 = bf16[32,4,128]{2,1,0:T(4,128)(2,1)S(1)} custom-call(bf16[64,8,128]{2,1,0:T(8,128)(2,1)S(1)} %all_to_all.30.recv_ref, bf16[512,256]{1,0:T(8,128)(2,1)S(1)} %copy-done.4, bf16[512,256]{1,0:T(8,128)(2,1)S(1)} %copy-done.3, bf16[256,512]{1,0:T(8,128)(2,1)S(1)} %copy-done.2, bf16[256,512]{1,0:T(8,128)(2,1)S(1)} %copy-done.1, ...), custom_call_target="tpu_custom_call" | custom-call | tf_op jit(solution)/shard_map/convolve/pallas_call | solution.py:272
  41.1 13.4 %all_to_all.31 = bf16[32,4,128]{2,1,0:T(4,128)(2,1)S(1)} all-to-all(bf16[32,4,128]{2,1,0:T(4,128)(2,1)S(1)} %convolve.1), channel_id=1, replica_groups={{336,344,352,360,368,376,320,328,464,472,480,488,496,504,448,456,80,88,..., dimensions={0} | all-to-all | bytes 65536 | tf_op jit(solution)/shard_map/all_to_all | solution.py:285
  54.5 11.7 %conditional.3 = (bf16[256,512]{1,0:T(8,128)(2,1)}) conditional(s32[]{:T(128)} %convert_element_type.4, (bf16[32,4,128]{2,1,0:T(4,128)(2,1)S(1)}, f32[32,512]{1,0:T(8,128)S(1)}, f32[32,512]{1,0:T(8,128)S(1)}, bf16[256,256]{1,0:T(8,128)(2,1)S(1)}) %tuple.18, (bf16[32,4,128]{2,1,0:T(4,128)(2,1)S(1)}, f32[32,512]{1,0:T(8,128)S(1)}, ...), branch_computations={%region_2.3_spmd, %region_3.4_spmd} | conditional | bytes 786440 | solution.py:307
  54.5 0.1 gate.3
  54.6 10.6 %all_to_all.29 = bf16[8,32,512]{2,1,0:T(8,128)(2,1)S(1)} all-to-all(bf16[8,32,512]{2,1,0:T(8,128)(2,1)S(1)} %gate.3), channel_id=1, replica_groups={{5,4,6,7,0,1,2,3},{13,12,14,15,8,9,10,11},{21,20,22,23,16,17,18,19},{29..., dimensions={0} | all-to-all | bytes 524288 | tf_op jit(solution)/shard_map/cond/branch_1_fun/all_to_all | solution.py:297
  65.2 1.0 %mix.3 = bf16[256,512]{1,0:T(8,128)(2,1)} custom-call(bf16[256,256]{1,0:T(8,128)(2,1)S(1)} %get-tuple-element.68.out_ref, bf16[256,512]{1,0:T(8,128)(2,1)S(1)} %bitcast.11), custom_call_target="tpu_custom_call" | custom-call | tf_op jit(solution)/shard_map/cond/branch_1_fun/mix/pallas_call | solution.py:298
Async XLA Ops:
  0.0 39.8 %copy-start.1 = (bf16[256,512]{1,0:T(8,128)(2,1)S(1)}, bf16[256,512]{1,0:T(8,128)(2,1)}, u32[]{:S(2)}) copy-start(bf16[256,512]{1,0:T(8,128)(2,1)} %constant.42.clone.back_lo) | copy-start | bytes 786436
  0.0 39.8 %copy-start.2 = (bf16[256,512]{1,0:T(8,128)(2,1)S(1)}, bf16[256,512]{1,0:T(8,128)(2,1)}, u32[]{:S(2)}) copy-start(bf16[256,512]{1,0:T(8,128)(2,1)} %constant.41.clone.back_hi) | copy-start | bytes 786436
  0.0 39.8 %copy-start.3 = (bf16[512,256]{1,0:T(8,128)(2,1)S(1)}, bf16[512,256]{1,0:T(8,128)(2,1)}, u32[]{:S(2)}) copy-start(bf16[512,256]{1,0:T(8,128)(2,1)} %constant.40.clone.fwd_lo) | copy-start | bytes 786436
  0.0 39.8 %copy-start.4 = (bf16[512,256]{1,0:T(8,128)(2,1)S(1)}, bf16[512,256]{1,0:T(8,128)(2,1)}, u32[]{:S(2)}) copy-start(bf16[512,256]{1,0:T(8,128)(2,1)} %constant.39.clone.fwd_hi) | copy-start | bytes 786436
  0.0 39.8 %copy-start.5 = (bf16[256,256]{1,0:T(8,128)(2,1)S(1)}, bf16[256,256]{1,0:T(8,128)(2,1)}, u32[]{:S(2)}) copy-start(bf16[256,256]{1,0:T(8,128)(2,1)} %constant.46.clone.out_lo) | copy-start | bytes 393220
  0.0 39.8 %copy-start.6 = (bf16[256,256]{1,0:T(8,128)(2,1)S(1)}, bf16[256,256]{1,0:T(8,128)(2,1)}, u32[]{:S(2)}) copy-start(bf16[256,256]{1,0:T(8,128)(2,1)} %constant.45.clone.out_hi) | copy-start | bytes 393220
  0.0 39.8 %copy-start.7 = (bf16[256,256]{1,0:T(8,128)(2,1)S(1)}, bf16[256,256]{1,0:T(8,128)(2,1)}, u32[]{:S(2)}) copy-start(bf16[256,256]{1,0:T(8,128)(2,1)} %constant.44.clone.in_lo) | copy-start | bytes 393220
  0.1 39.8 %copy-start.8 = (bf16[256,256]{1,0:T(8,128)(2,1)S(1)}, bf16[256,256]{1,0:T(8,128)(2,1)}, u32[]{:S(2)}) copy-start(bf16[256,256]{1,0:T(8,128)(2,1)} %constant.43.clone.in_hi) | copy-start | bytes 393220
  17.8 22.1 %copy-start = (f32[2,256,128]{2,1,0:T(8,128)S(1)}, f32[2,256,128]{2,1,0:T(8,128)}, u32[]{:S(2)}) copy-start(f32[2,256,128]{2,1,0:T(8,128)} %constant.47.clone.twist_ref) | copy-start | bytes 786436
